TPU v7x, 512 devices: a whole 4x8x8 slice. The times are simulated.
512 devices in a mesh: cent: 8 (over z), pts: 64 (over x, y, core).
Axes of the slice: x: 4, y: 8, z: 8, core: 2. Of those that a mesh axis runs over, the one named last changes fastest.
Arguments:
- points: bfloat16 [65536, 1024], P('pts'), may hold values from -120 to 120
- centroids: bfloat16 [4096, 1024], P(('cent', 'pts')), may hold values from -4 to 4
Outputs:
- new_centroids: bfloat16 [4096, 1024], P(('cent', 'pts'))
- lse: float32 [65536], P('pts')
All inputs are finite; a program needn't handle non-finite values.
Results may differ from a plain program's by a relative error of at most 0.006.
Values may be sent and summed in bfloat16 or wider, within the bound.
No kernel may reach another device: no remote copies, remote signals or barrier semaphores. Data moves between devices by JAX's collectives and lax.ppermute only.
A program may use at most 64 MiB of HBM per device.

v0:
```python
import math

import jax
import jax.numpy as jnp
from jax import lax
from jax.sharding import PartitionSpec as P


def body(points, centroids):
    scale = 2.0 / math.sqrt(points.shape[1])
    group = lax.all_gather(centroids, "pts", axis=0, tiled=True)
    group_f = group.astype(jnp.float32)
    sq_norms = jnp.sum(group_f * group_f, axis=1)
    logits = (
        jnp.dot(points, group.T, preferred_element_type=jnp.float32) - 0.5 * sq_norms[None, :]
    ) * scale
    local_max = jnp.max(logits, axis=1)
    local_sum = jnp.sum(jnp.exp(logits - local_max[:, None]), axis=1)
    top = lax.pmax(local_max, "cent")
    total = lax.psum(local_sum * jnp.exp(local_max - top), "cent")
    lse = top + jnp.log(total)
    resp = jnp.exp(logits - lse[:, None]).astype(jnp.bfloat16)
    sums = lax.dot_general(
        resp, points, (((0,), (0,)), ((), ())), preferred_element_type=jnp.float32
    )
    mass = jnp.sum(resp.astype(jnp.float32), axis=0)
    owned = centroids.shape[0]
    all_sums, all_mass = lax.psum((sums, mass), "pts")
    start = lax.axis_index("pts") * owned
    own_sums = lax.dynamic_slice_in_dim(all_sums, start, owned, 0)
    own_mass = lax.dynamic_slice_in_dim(all_mass, start, owned, 0)
    updated = (own_sums + centroids.astype(jnp.float32)) / (own_mass[:, None] + 1.0)
    return (updated.astype(jnp.bfloat16), lse)


def solution(mesh):
    placed = (P("pts", None), P(("cent", "pts"), None))
    return jax.shard_map(
        body,
        mesh=mesh,
        in_specs=placed,
        out_specs=(P(("cent", "pts"), None), P("pts")),
        check_vma=False,
    )
```

profile of v0, /device:TPU:6, one launch (start us, length us, event | category | flops | bytes accessed | tf_op | source)
XLA Modules:
  0.0 345.4 jit_solution(9739695912173881714)
XLA Ops:
  7.2 0.0 copy-start
  7.2 0.0 all-gather.2.cloned.1.call-start
  7.2 0.7 all-gather.2.cloned.1.call-update
  7.9 0.0 all-reduce.2.cloned.1.call-start
  8.0 88.5 %all-gather.2.cloned.1.call-done = bf16[512,1024]{1,0:T(8,128)(2,1)} async-done(((bf16[8,1024]{1,0:T(8,128)(2,1)}), bf16[512,1024]{1,0:T(8,128)(2,1)}) %all-gather.2.cloned.1.call-update) | async-done | bytes 1048592 | tf_op jit(solution)/shard_map/all_gather | solution.py:11
  96.5 1.5 multiply_reduce_fusion
  98.0 0.0 copy-done
  98.0 3.9 %fusion = (f32[1024]{0:T(1024)S(1)}, f32[1024,512]{0,1:T(8,128)}) fusion(f32[512]{0:T(512)S(1)} %broadcast_multiply_fusion, bf16[1024,1024]{1,0:T(8,128)(2,1)S(1)} %copy-done, bf16[512,1024]{1,0:T(8,128)(2,1)} %all-gather.2.cloned.1.call-done), kind=kOutput, calls=%fused_computation.5 | convolution fusion | flops 1075313664 | bytes 5249024 | tf_op jit(solution)/shard_map/dot_general | solution.py:15
  101.9 18.1 %pmax.7 = f32[1024]{0:T(1024)S(1)} all-reduce(f32[1024]{0:T(1024)S(1)} %get-tuple-element.2), channel_id=1, replica_groups=mesh['cent'=8,'pts'=64] {'cent'}, use_global_device_ids=true, to_apply=%region_2.0 | all-reduce | flops 1024 | bytes 8192 | tf_op jit(solution)/shard_map/pmax | solution.py:19
  120.0 2.1 exponential_reduce_fusion
  122.1 14.8 %psum.21 = f32[1024]{0:T(1024)S(1)} all-reduce(f32[1024]{0:T(1024)S(1)} %exponential_multiply_fusion), channel_id=1, replica_groups=mesh['cent'=8,'pts'=64] {'cent'}, use_global_device_ids=true, to_apply=%region_4.0 | all-reduce | flops 1024 | bytes 8192 | tf_op jit(solution)/shard_map/psum | solution.py:20
  136.8 0.0 copy-start.2
  136.8 4.3 %fusion.1 = f32[512,1024]{1,0:T(8,128)} fusion(bf16[1024,1024]{1,0:T(8,128)(2,1)S(1)} %copy-done, f32[1024,512]{0,1:T(8,128)} %get-tuple-element.3, f32[1024]{0:T(1024)S(1)} %log_add_fusion, f32[512]{0:T(512)S(1)} %broadcast_multiply_fusion), kind=kOutput, calls=%fused_computation.11 | convolution fusion | flops 1075838976 | bytes 6297600 | tf_op jit(solution)/shard_map/dot_general | solution.py:23
  141.1 0.0 copy-start.1
  141.1 0.0 all-reduce.2.cloned.1.call-update
  141.1 0.0 copy-done.2
  141.2 2.2 convert_reduce_fusion
  143.4 104.7 %psum.23 = f32[512]{0:T(512)S(1)} all-reduce(f32[512]{0:T(512)S(1)} %convert_reduce_fusion), channel_id=1, replica_groups=mesh['cent'=8,'pts'=64] {'pts'}, use_global_device_ids=true, to_apply=%region_7.0 | all-reduce | flops 512 | bytes 4096 | tf_op jit(solution)/shard_map/psum | solution.py:28
  248.1 0.1 dynamic-slice_add_fusion
  248.1 89.0 %all-reduce.2.cloned.1.call-done = f32[512,1024]{1,0:T(8,128)} async-done(((f32[512,1024]{1,0:T(8,128)}), f32[512,1024]{1,0:T(8,128)}) %all-reduce.2.cloned.1.call-update) | async-done | bytes 2097168 | tf_op jit(solution)/shard_map/psum | solution.py:28
  337.1 0.0 copy-done.1
  337.1 1.4 divide_convert_fusion
  (3 shorter events, 0.0 us)
Async XLA Ops:
  7.2 90.8 %copy-start = (bf16[1024,1024]{1,0:T(8,128)(2,1)S(1)}, bf16[1024,1024]{1,0:T(8,128)(2,1)}, u32[]{:S(2)}) copy-start(bf16[1024,1024]{1,0:T(8,128)(2,1)} %param.2) | copy-start | bytes 6291460
  7.2 89.3 %all-gather.2.cloned.1.call-start = ((), (), s32[]{:S(2)}) async-start(), calls=%async_computation | async-start | bytes 1064960 | tf_op jit(solution)/shard_map/all_gather | solution.py:11
  7.9 329.2 %all-reduce.2.cloned.1.call-start = ((), (), s32[]{:S(2)}) async-start(), calls=%async_computation.1 | async-start | bytes 4194304 | tf_op jit(solution)/shard_map/psum | solution.py:28
  136.8 4.3 %copy-start.2 = (f32[1024]{0:T(1024)}, f32[1024]{0:T(1024)S(1)}, u32[]{:S(2)}) copy-start(f32[1024]{0:T(1024)S(1)} %log_add_fusion) | copy-start | bytes 12292
  141.1 196.0 %copy-start.1 = (bf16[8,1024]{1,0:T(8,128)(2,1)S(1)}, bf16[8,1024]{1,0:T(8,128)(2,1)}, u32[]{:S(2)}) copy-start(bf16[8,1024]{1,0:T(8,128)(2,1)} %param.3) | copy-start | bytes 49156
Sparse Core Ops, SparseCore 0:
  11.4 85.0 all-gather.1
  141.3 195.8 all-reduce.1
where the time goes:
time: 348 us; the launch traced here: 345 us
  waiting for transfers between devices  178 us (51%)
  blocking collectives  138 us (40%)
  between operations  14.1 us (4%)
  matrix products  8.13 us (2%)
  other arithmetic  7.33 us (2%)
    psum x1, blocking collectives, body(): all_sums, all_mass = lax.psum((sums, mass), 'pts')  105 us
    psum x1, waiting for transfers between devices, body(): all_sums, all_mass = lax.psum((sums, mass), 'pts')  89 us
    all_gather x1, waiting for transfers between devices, body(): group = lax.all_gather(centroids, 'pts', axis=0, tiled=True)  88.5 us
    pmax x1, blocking collectives, body(): top = lax.pmax(local_max, 'cent')  18.1 us
    psum x1, blocking collectives, body(): total = lax.psum(local_sum * jnp.exp(local_max - top), 'cent')  14.8 us
  transfers between devices with their start and end apart: 2, of which 2 were waited for; matrix products, arithmetic and copies ran while one was open for 1% of the time, Pallas kernels for 0%

commit v1 on v0

v1 whole, which is shorter than its diff:
```python
import functools
import math

import jax
import jax.numpy as jnp
from jax import lax
from jax.experimental import pallas as pl
from jax.experimental.pallas import tpu as pltpu
from jax.sharding import Mesh, PartitionSpec as P

LANES = 128
CORES = 2
VMEM_LIMIT = 40 * 1024 * 1024
F32 = jnp.float32
BF16 = jnp.bfloat16


def in_vmem(x):
    return pltpu.with_memory_space_constraint(x, pltpu.VMEM)


def whole(n):
    return [pl.BlockSpec(memory_space=pltpu.VMEM)] * n


def local_kernel(scale, core_ref, group_ref, own_ref, other_ref, logits_ref, part_ref):
    group = group_ref[...]
    group_f = group.astype(F32)
    half_norms = 0.5 * jnp.sum(group_f * group_f, axis=1, keepdims=True)
    core = core_ref[0]
    points = own_ref.shape[0]
    width = 2 * LANES
    for which, ref in enumerate((own_ref, other_ref)):
        rows = []
        for start in range(0, points, width):
            dots = lax.dot_general(
                group, ref[pl.ds(start, width), :], (((1,), (1,)), ((), ())), preferred_element_type=F32
            )
            logits = (dots - half_norms) * scale
            logits_ref[which, :, pl.ds(start, width)] = logits
            top = jnp.max(logits, axis=0, keepdims=True)
            lse = top + jnp.log(jnp.sum(jnp.exp(logits - top), axis=0, keepdims=True))
            rows += [lse[:, i : i + LANES] for i in range(0, width, LANES)]
        block = jnp.concatenate(rows, axis=0)
        count = block.shape[0]
        place = pl.multiple_of((core if which == 0 else 1 - core) * count, count)
        for peer in range(part_ref.shape[0]):
            part_ref[peer, pl.ds(place, count), :] = block


def sums_kernel(core_ref, logits_ref, parts_ref, own_ref, other_ref, send_ref, lse_ref, resp_ref, total_ref):
    parts = parts_ref[...]
    top = jnp.max(parts, axis=0)
    total_ref[...] = top + jnp.log(jnp.sum(jnp.exp(parts - top[None]), axis=0))
    core = core_ref[0]
    points, width = own_ref.shape
    count = points // LANES
    mass = jnp.zeros((logits_ref.shape[1], LANES), F32)
    for which in range(CORES):
        place = pl.multiple_of((core if which == 0 else 1 - core) * count, count)
        lse = total_ref[pl.ds(place, count), :]
        if which == 0:
            lse_ref[...] = lse
        for i in range(count):
            cols = pl.ds(i * LANES, LANES)
            resp = jnp.exp(logits_ref[which, :, cols] - lse[i : i + 1, :]).astype(BF16)
            resp_ref[which, :, cols] = resp
            mass += resp.astype(F32)
    mass = jnp.sum(mass, axis=1, keepdims=True)
    high = mass.astype(BF16).astype(F32)
    lane = lax.broadcasted_iota(jnp.int32, (mass.shape[0], LANES), 1)
    send_ref[:, pl.ds(width, LANES)] = jnp.where(lane < LANES // 2, high, mass - high).astype(BF16)
    step = 2 * LANES
    for start in range(0, width, step):
        cols = pl.ds(start, step)
        sums = jnp.dot(resp_ref[0], own_ref[:, cols], preferred_element_type=F32)
        sums += jnp.dot(resp_ref[1], other_ref[:, cols], preferred_element_type=F32)
        send_ref[:, cols] = sums.astype(BF16)


def update_kernel(got_ref, cent_ref, out_ref):
    own, width = cent_ref.shape
    step = 2 * own
    total = got_ref[pl.ds(0, step), :].astype(F32)
    for start in range(step, got_ref.shape[0], step):
        total += got_ref[pl.ds(start, step), :].astype(F32)
    total = total[:own] + total[own:]
    mass = total[:, width : width + 1] + total[:, width + LANES // 2 : width + LANES // 2 + 1]
    out_ref[...] = ((total[:, :width] + cent_ref[...].astype(F32)) / (mass + 1.0)).astype(BF16)


def body(points, centroids):
    rows, width = points.shape
    own = centroids.shape[0]
    chips = lax.axis_size("chip")
    groups = lax.axis_size("cent") * CORES
    rank = own * chips
    params = pltpu.CompilerParams(vmem_limit_bytes=VMEM_LIMIT)
    smem = pl.BlockSpec(memory_space=pltpu.SMEM)
    core = lax.axis_index("core").astype(jnp.int32).reshape(1)

    other = lax.ppermute(points, "core", [(0, 1), (1, 0)])
    sent = jnp.broadcast_to(centroids[None], (chips, own, width))
    group = lax.all_to_all(sent, "chip", 0, 0).reshape(rank, width)

    logits, part = pl.pallas_call(
        functools.partial(local_kernel, 2.0 / math.sqrt(width)),
        out_shape=(
            pltpu.VMEM((CORES, rank, rows), F32),
            jax.ShapeDtypeStruct((groups, CORES * rows // LANES, LANES), F32),
        ),
        in_specs=[smem] + whole(3),
        out_specs=tuple(whole(2)),
        compiler_params=params,
        name="local",
    )(core, in_vmem(group), in_vmem(points), in_vmem(other))

    parts = lax.all_to_all(part, ("cent", "core"), 0, 0)

    send, lse = pl.pallas_call(
        sums_kernel,
        out_shape=(
            jax.ShapeDtypeStruct((rank, width + LANES), BF16),
            jax.ShapeDtypeStruct((rows // LANES, LANES), F32),
        ),
        in_specs=[smem] + whole(4),
        out_specs=tuple(whole(2)),
        scratch_shapes=[
            pltpu.VMEM((CORES, rank, rows), BF16),
            pltpu.VMEM((CORES * rows // LANES, LANES), F32),
        ],
        compiler_params=params,
        name="sums",
    )(core, in_vmem(logits), in_vmem(parts), in_vmem(points), in_vmem(other))

    got = lax.all_to_all(send.reshape(chips, own, width + LANES), "chip", 0, 0)

    updated = pl.pallas_call(
        update_kernel,
        out_shape=jax.ShapeDtypeStruct((own, width), BF16),
        in_specs=whole(2),
        out_specs=whole(1)[0],
        compiler_params=params,
        name="update",
    )(in_vmem(got.reshape(rank, width + LANES)), centroids)
    return updated, lse.reshape(rows)


def solution(mesh):
    cent, pts = mesh.shape["cent"], mesh.shape["pts"]
    fine = Mesh(mesh.devices.reshape(cent, pts // CORES, CORES), ("cent", "chip", "core"))
    spread = P(("cent", "chip", "core"), None)
    return jax.shard_map(
        body,
        mesh=fine,
        in_specs=(P(("chip", "core"), None), spread),
        out_specs=(spread, P(("chip", "core"))),
        check_vma=False,
    )
```

time: 348 us -> 81.9 us (0.24)
  the two profiles are of different devices: /device:TPU:6 before, /device:TPU:8 now
where the time goes in v1:
time: 81.9 us; the launch traced here: 81.5 us
  blocking collectives  43.4 us (53%)
  waiting for transfers between devices  18.3 us (22%)
  starting transfers between devices  12.1 us (15%)
  Pallas kernels  3.92 us (5%)
  local copies, waits for them, and re-layouts  3.17 us (4%)
    all_to_all x1, blocking collectives, body(): got = lax.all_to_all(send.reshape(chips, own, width + LANES), 'chip', 0, 0)  24.4 us
    all_to_all x1, blocking collectives, body(): parts = lax.all_to_all(part, ('cent', 'core'), 0, 0)  19 us
    all_to_all x1, waiting for transfers between devices, body(): group = lax.all_to_all(sent, 'chip', 0, 0).reshape(rank, width)  18.3 us
    all_to_all x1, starting transfers between devices, body(): group = lax.all_to_all(sent, 'chip', 0, 0).reshape(rank, width)  10.2 us
    ppermute x1, starting transfers between devices, body(): other = lax.ppermute(points, 'core', [(0, 1), (1, 0)])  1.92 us
    pallas_call x1, Pallas kernels, body(): pl.pallas_call(functools.partial(local_kernel, 2.0 / math.sqrt(width)), o...  1.73 us
  transfers between devices with their start and end apart: 2, of which 1 were waited for; matrix products, arithmetic and copies ran while one was open for 2% of the time, Pallas kernels for 0%

profile of v1, /device:TPU:8, one launch (start us, length us, event | category | flops | bytes accessed | tf_op | source)
XLA Modules:
  0.0 81.5 jit_solution(13166164899876763883)
XLA Ops:
  0.6 1.9 %collective-permute-start = (bf16[1024,1024]{1,0:T(8,128)(2,1)}, bf16[1024,1024]{1,0:T(8,128)(2,1)S(1)}, u32[]{:S(2)}, u32[]{:S(2)}) collective-permute-start(bf16[1024,1024]{1,0:T(8,128)(2,1)} %own_ref.3), channel_id=1, source_target_pairs={{0,1},{1,0},{2,3},{3,2},{4,5},{5,4},{6,7},{7,6},{8,9},{9,8},{10,11... | collective-permute-start | bytes 6291464 | tf_op jit(solution)/shard_map/ppermute | solution.py:102
  2.6 1.6 %broadcast_in_dim.2 = bf16[32,8,1024]{2,1,0:T(8,128)(2,1)} broadcast(bf16[8,1024]{1,0:T(8,128)(2,1)} %cent_ref.1), dimensions={1,2} | broadcast | bytes 540672 | tf_op jit(solution)/shard_map/broadcast_in_dim | solution.py:103
  4.1 10.2 %all-to-all-start = ((bf16[32,8,1024]{2,1,0:T(8,128)(2,1)}), bf16[32,8,1024]{2,1,0:T(8,128)(2,1)S(1)}, u32[]{:S(2)}, u32[]{:S(2)}) async-start(bf16[32,8,1024]{2,1,0:T(8,128)(2,1)} %broadcast_in_dim.2), calls=%async_computation | async-start | bytes 1048576 | tf_op jit(solution)/shard_map/all_to_all | solution.py:104
  14.3 18.3 %all-to-all-done = bf16[32,8,1024]{2,1,0:T(8,128)(2,1)S(1)} async-done(((bf16[32,8,1024]{2,1,0:T(8,128)(2,1)}), bf16[32,8,1024]{2,1,0:T(8,128)(2,1)S(1)}, u32[]{:S(2)}, u32[]{:S(2)}) %all-to-all-start) | async-done | bytes 524320 | tf_op jit(solution)/shard_map/all_to_all | solution.py:104
  32.6 0.0 collective-permute-done.other_ref
  32.6 0.0 copy-start
  32.6 1.6 %copy-done = bf16[1024,1024]{1,0:T(8,128)(2,1)S(1)} copy-done((bf16[1024,1024]{1,0:T(8,128)(2,1)S(1)}, bf16[1024,1024]{1,0:T(8,128)(2,1)}, u32[]{:S(2)}) %copy-start) | copy-done | bytes 2097176
  34.2 0.0 copy-start.1
  34.2 1.7 %local.1 = (f32[2,256,1024]{2,1,0:T(8,128)S(1)}, f32[16,16,128]{2,1,0:T(8,128)S(1)}) custom-call(s32[1]{0:T(128)} %bitcast.core_ref, bf16[256,1024]{1,0:T(8,128)(2,1)S(1)} %bitcast.6, bf16[1024,1024]{1,0:T(8,128)(2,1)S(1)} %copy-done, bf16[1024,1024]{1,0:T(8,128)(2,1)S(1)} %collective-permute-done.other_ref), custom_call_target="tpu_custom_call" | custom-call | tf_op jit(solution)/shard_map/local/pallas_call | solution.py:106
  35.9 19.0 %all_to_all.15.parts_ref = f32[16,16,128]{2,1,0:T(8,128)S(1)} all-to-all(f32[16,16,128]{2,1,0:T(8,128)S(1)} %get-tuple-element.7), channel_id=1, replica_groups=mesh['cent'=8,'chip'=32,'core'=2] {'cent','core'}, dimensions={0} | all-to-all | bytes 262144 | tf_op jit(solution)/shard_map/all_to_all | solution.py:118
  54.9 0.0 copy-done.1
  54.9 0.0 copy-start.2
  54.9 1.4 %sums.1 = (bf16[256,1152]{1,0:T(8,128)(2,1)S(1)}, f32[8,128]{1,0:T(8,128)}) custom-call(s32[1]{0:T(128)} %bitcast.core_ref, f32[2,256,1024]{2,1,0:T(8,128)S(1)} %get-tuple-element.6.logits_ref, f32[16,16,128]{2,1,0:T(8,128)S(1)} %all_to_all.15.parts_ref, bf16[1024,1024]{1,0:T(8,128)(2,1)S(1)} %copy-done.1, bf16[1024,1024]{1,0:T(8,128)(2,1)S(1)} %collective-permute-done.other_ref), custom_call_target="tpu_custom_call" | custom-call | tf_op jit(solution)/shard_map/sums/pallas_call | solution.py:120
  56.3 24.4 %all_to_all.16 = bf16[32,8,1152]{2,1,0:T(8,128)(2,1)S(1)} all-to-all(bf16[32,8,1152]{2,1,0:T(8,128)(2,1)S(1)} %bitcast.7), channel_id=1, replica_groups=mesh['cent'=8,'chip'=32,'core'=2] {'chip'}, dimensions={0} | all-to-all | bytes 1179648 | tf_op jit(solution)/shard_map/all_to_all | solution.py:136
  80.7 0.0 copy-done.2
  80.7 0.8 update.1
Async XLA Ops:
  0.6 32.0 %collective-permute-start = (bf16[1024,1024]{1,0:T(8,128)(2,1)}, bf16[1024,1024]{1,0:T(8,128)(2,1)S(1)}, u32[]{:S(2)}, u32[]{:S(2)}) collective-permute-start(bf16[1024,1024]{1,0:T(8,128)(2,1)} %own_ref.3), channel_id=1, source_target_pairs={{0,1},{1,0},{2,3},{3,2},{4,5},{5,4},{6,7},{7,6},{8,9},{9,8},{10,11... | collective-permute-start | bytes 6291464 | tf_op jit(solution)/shard_map/ppermute | solution.py:102
  4.1 28.5 %all-to-all-start = ((bf16[32,8,1024]{2,1,0:T(8,128)(2,1)}), bf16[32,8,1024]{2,1,0:T(8,128)(2,1)S(1)}, u32[]{:S(2)}, u32[]{:S(2)}) async-start(bf16[32,8,1024]{2,1,0:T(8,128)(2,1)} %broadcast_in_dim.2), calls=%async_computation | async-start | bytes 1048576 | tf_op jit(solution)/shard_map/all_to_all | solution.py:104
  32.6 1.6 %copy-start = (bf16[1024,1024]{1,0:T(8,128)(2,1)S(1)}, bf16[1024,1024]{1,0:T(8,128)(2,1)}, u32[]{:S(2)}) copy-start(bf16[1024,1024]{1,0:T(8,128)(2,1)} %own_ref.3) | copy-start | bytes 6291460
  34.2 20.7 %copy-start.1 = (bf16[1024,1024]{1,0:T(8,128)(2,1)S(1)}, bf16[1024,1024]{1,0:T(8,128)(2,1)}, u32[]{:S(2)}) copy-start(bf16[1024,1024]{1,0:T(8,128)(2,1)} %own_ref.3) | copy-start | bytes 6291460
  54.9 25.8 %copy-start.2 = (bf16[8,1024]{1,0:T(8,128)(2,1)S(1)}, bf16[8,1024]{1,0:T(8,128)(2,1)}, u32[]{:S(2)}) copy-start(bf16[8,1024]{1,0:T(8,128)(2,1)} %cent_ref.1) | copy-start | bytes 49156

commit v2 on v1

--- a/solution.py
+++ b/solution.py
@@ -23,16 +23,22 @@
     return [pl.BlockSpec(memory_space=pltpu.VMEM)] * n
 
 
-def local_kernel(scale, core_ref, group_ref, own_ref, other_ref, logits_ref, part_ref):
-    group = group_ref[...]
-    group_f = group.astype(F32)
-    half_norms = 0.5 * jnp.sum(group_f * group_f, axis=1, keepdims=True)
+def local_kernel(scale, core_ref, group_ref, other_ref, from_ref, logits_ref, part_ref, own_ref, sems):
+    step = own_ref.shape[0] // sems.shape[0]
+    copies = []
+    for i in range(sems.shape[0]):
+        part = pl.ds(i * step, step)
+        copies.append(pltpu.make_async_copy(from_ref.at[part, :], own_ref.at[part, :], sems.at[i]))
+        copies[-1].start()
     core = core_ref[0]
-    points = own_ref.shape[0]
-    width = 2 * LANES
-    for which, ref in enumerate((own_ref, other_ref)):
+
+    def half(which, ref):
+        group = group_ref[...]
+        group_f = group.astype(F32)
+        half_norms = 0.5 * jnp.sum(group_f * group_f, axis=1, keepdims=True)
+        width = 2 * LANES
         rows = []
-        for start in range(0, points, width):
+        for start in range(0, ref.shape[0], width):
             dots = lax.dot_general(
                 group, ref[pl.ds(start, width), :], (((1,), (1,)), ((), ())), preferred_element_type=F32
             )
@@ -46,6 +52,17 @@
         place = pl.multiple_of((core if which == 0 else 1 - core) * count, count)
         for peer in range(part_ref.shape[0]):
             part_ref[peer, pl.ds(place, count), :] = block
+
+    @pl.when(core >= 0)
+    def _():
+        half(1, other_ref)
+
+    for copy in copies:
+        copy.wait()
+
+    @pl.when(core >= 0)
+    def _():
+        half(0, own_ref)
 
 
 def sums_kernel(core_ref, logits_ref, parts_ref, own_ref, other_ref, send_ref, lse_ref, resp_ref, total_ref):
@@ -100,20 +117,22 @@
     core = lax.axis_index("core").astype(jnp.int32).reshape(1)
 
     other = lax.ppermute(points, "core", [(0, 1), (1, 0)])
-    sent = jnp.broadcast_to(centroids[None], (chips, own, width))
+    sent, core = lax.optimization_barrier((jnp.broadcast_to(centroids[None], (chips, own, width)), core))
     group = lax.all_to_all(sent, "chip", 0, 0).reshape(rank, width)
 
-    logits, part = pl.pallas_call(
+    logits, part, points = pl.pallas_call(
         functools.partial(local_kernel, 2.0 / math.sqrt(width)),
         out_shape=(
             pltpu.VMEM((CORES, rank, rows), F32),
             jax.ShapeDtypeStruct((groups, CORES * rows // LANES, LANES), F32),
+            pltpu.VMEM((rows, width), BF16),
         ),
-        in_specs=[smem] + whole(3),
-        out_specs=tuple(whole(2)),
+        in_specs=[smem] + whole(2) + [pl.BlockSpec(memory_space=pl.ANY)],
+        out_specs=tuple(whole(3)),
+        scratch_shapes=[pltpu.SemaphoreType.DMA((4,))],
         compiler_params=params,
         name="local",
-    )(core, in_vmem(group), in_vmem(points), in_vmem(other))
+    )(core, in_vmem(group), in_vmem(other), pltpu.with_memory_space_constraint(points, pltpu.HBM))
 
     parts = lax.all_to_all(part, ("cent", "core"), 0, 0)
 

time: 81.9 us -> 80.1 us (0.978)
  blocking collectives: 43.4 us -> 71.6 us
  waiting for transfers between devices: 18.3 us -> 0.01 us
  starting transfers between devices: 12.1 us -> 1.92 us
  local copies, waits for them, and re-layouts: 3.17 us -> 0.77 us
    all_to_all x0 -> x1, blocking collectives: none -> 28.3 us  [body(): group = lax.all_to_all(sent, 'chip', 0, 0).reshape(rank, width)]
    all_to_all x1 -> x0, waiting for transfers between devices: 18.3 us -> none  [body(): group = lax.all_to_all(sent, 'chip', 0, 0).reshape(rank, width)]
    all_to_all x1 -> x0, starting transfers between devices: 10.2 us -> none  [body(): group = lax.all_to_all(sent, 'chip', 0, 0).reshape(rank, width)]
    unnamed x6 -> x2, local copies, waits for them, and re-layouts: 1.6 us -> 0.01 us
  transfers between devices with their start and end apart: 2 -> 1, of which waited for: 1 -> 0; matrix products, arithmetic and copies ran while one was open for 2% -> 1% of each run, Pallas kernels for 0% -> 0%
where the time goes in v2:
time: 80.1 us; the launch traced here: 79.7 us
  blocking collectives  71.6 us (89%)
  Pallas kernels  4.73 us (6%)
  starting transfers between devices  1.92 us (2%)
    all_to_all x1, blocking collectives, body(): group = lax.all_to_all(sent, 'chip', 0, 0).reshape(rank, width)  28.3 us
    all_to_all x1, blocking collectives, body(): got = lax.all_to_all(send.reshape(chips, own, width + LANES), 'chip', 0, 0)  24.4 us
    all_to_all x1, blocking collectives, body(): parts = lax.all_to_all(part, ('cent', 'core'), 0, 0)  19 us
    pallas_call x1, Pallas kernels, body(): pl.pallas_call(functools.partial(local_kernel, 2.0 / math.sqrt(width)), o...  2.54 us
    ppermute x1, starting transfers between devices, body(): other = lax.ppermute(points, 'core', [(0, 1), (1, 0)])  1.92 us
  transfers between devices with their start and end apart: 1, of which 0 were waited for; matrix products, arithmetic and copies ran while one was open for 1% of the time, Pallas kernels for 0%

profile of v2, /device:TPU:8, one launch (start us, length us, event | category | flops | bytes accessed | tf_op | source)
XLA Modules:
  0.0 79.7 jit_solution(5037692468345746211)
XLA Ops:
  0.6 1.9 %collective-permute-start = (bf16[1024,1024]{1,0:T(8,128)(2,1)}, bf16[1024,1024]{1,0:T(8,128)(2,1)S(1)}, u32[]{:S(2)}, u32[]{:S(2)}) collective-permute-start(bf16[1024,1024]{1,0:T(8,128)(2,1)} %from_ref.1), channel_id=1, source_target_pairs={{0,1},{1,0},{2,3},{3,2},{4,5},{5,4},{6,7},{7,6},{8,9},{9,8},{10,11... | collective-permute-start | bytes 6291464 | tf_op jit(solution)/shard_map/ppermute | solution.py:119
  2.6 0.8 broadcast_in_dim.2
  3.3 28.3 %all_to_all.15 = bf16[32,8,1024]{2,1,0:T(8,128)(2,1)S(1)} all-to-all(bf16[32,8,1024]{2,1,0:T(8,128)(2,1)S(1)} %broadcast_in_dim.2), channel_id=1, replica_groups=mesh['cent'=8,'chip'=32,'core'=2] {'chip'}, dimensions={0} | all-to-all | bytes 1048576 | tf_op jit(solution)/shard_map/all_to_all | solution.py:121
  31.6 0.0 collective-permute-done.other_ref
  31.6 2.5 %local.1 = (f32[2,256,1024]{2,1,0:T(8,128)S(1)}, f32[16,16,128]{2,1,0:T(8,128)S(1)}, bf16[1024,1024]{1,0:T(8,128)(2,1)S(1)}) custom-call(s32[1]{0:T(128)} %bitcast.core_ref, bf16[256,1024]{1,0:T(8,128)(2,1)S(1)} %bitcast.6, bf16[1024,1024]{1,0:T(8,128)(2,1)S(1)} %collective-permute-done.other_ref, bf16[1024,1024]{1,0:T(8,128)(2,1)} %from_ref.1), custom_call_target="tpu_custom_call" | custom-call | tf_op jit(solution)/shard_map/local/pallas_call | solution.py:123
  34.2 19.0 %all_to_all.16.parts_ref = f32[16,16,128]{2,1,0:T(8,128)S(1)} all-to-all(f32[16,16,128]{2,1,0:T(8,128)S(1)} %get-tuple-element.12), channel_id=1, replica_groups=mesh['cent'=8,'chip'=32,'core'=2] {'cent','core'}, dimensions={0} | all-to-all | bytes 262144 | tf_op jit(solution)/shard_map/all_to_all | solution.py:137
  53.1 0.0 copy-start
  53.1 1.4 %sums.1 = (bf16[256,1152]{1,0:T(8,128)(2,1)S(1)}, f32[8,128]{1,0:T(8,128)}) custom-call(s32[1]{0:T(128)} %bitcast.core_ref, f32[2,256,1024]{2,1,0:T(8,128)S(1)} %get-tuple-element.11.logits_ref, f32[16,16,128]{2,1,0:T(8,128)S(1)} %all_to_all.16.parts_ref, bf16[1024,1024]{1,0:T(8,128)(2,1)S(1)} %get-tuple-element.13.own_ref, ...), custom_call_target="tpu_custom_call" | custom-call | tf_op jit(solution)/shard_map/sums/pallas_call | solution.py:139
  54.5 24.4 %all_to_all.17 = bf16[32,8,1152]{2,1,0:T(8,128)(2,1)S(1)} all-to-all(bf16[32,8,1152]{2,1,0:T(8,128)(2,1)S(1)} %bitcast.7), channel_id=1, replica_groups=mesh['cent'=8,'chip'=32,'core'=2] {'chip'}, dimensions={0} | all-to-all | bytes 1179648 | tf_op jit(solution)/shard_map/all_to_all | solution.py:155
  79.0 0.0 copy-done
  79.0 0.8 update.1
Async XLA Ops:
  0.6 31.0 %collective-permute-start = (bf16[1024,1024]{1,0:T(8,128)(2,1)}, bf16[1024,1024]{1,0:T(8,128)(2,1)S(1)}, u32[]{:S(2)}, u32[]{:S(2)}) collective-permute-start(bf16[1024,1024]{1,0:T(8,128)(2,1)} %from_ref.1), channel_id=1, source_target_pairs={{0,1},{1,0},{2,3},{3,2},{4,5},{5,4},{6,7},{7,6},{8,9},{9,8},{10,11... | collective-permute-start | bytes 6291464 | tf_op jit(solution)/shard_map/ppermute | solution.py:119
  53.1 25.8 %copy-start = (bf16[8,1024]{1,0:T(8,128)(2,1)S(1)}, bf16[8,1024]{1,0:T(8,128)(2,1)}, u32[]{:S(2)}) copy-start(bf16[8,1024]{1,0:T(8,128)(2,1)} %cent_ref.1) | copy-start | bytes 49156

commit v3 on v2

v3 whole, which is shorter than its diff:
```python
import functools
import math

import jax
import jax.numpy as jnp
from jax import lax
from jax.experimental import pallas as pl
from jax.experimental.pallas import tpu as pltpu
from jax.sharding import Mesh, PartitionSpec as P

LANES = 128
CORES = 2
ACROSS = 4
PIECES = 4
STAGE_FLOPS = 10**10
VMEM_LIMIT = 40 * 1024 * 1024
F32 = jnp.float32
BF16 = jnp.bfloat16


def in_vmem(x):
    return pltpu.with_memory_space_constraint(x, pltpu.VMEM)


def whole(n):
    return [pl.BlockSpec(memory_space=pltpu.VMEM)] * n


def stage_kernel(points_ref, *refs):
    *out_refs, sems = refs
    copies, place = [], 0
    for i, ref in enumerate(out_refs):
        copies.append(pltpu.make_async_copy(points_ref.at[pl.ds(place, ref.shape[0]), :], ref, sems.at[i]))
        copies[-1].start()
        place += ref.shape[0]
    for copy in copies:
        copy.wait()


def local_kernel(scale, core_ref, group_ref, *refs):
    own_refs, from_refs = refs[:PIECES], refs[PIECES : 2 * PIECES]
    logits_ref, part_ref, other_ref, held_ref, sems = refs[2 * PIECES :]
    copies, place = [], 0
    for i, ref in enumerate(from_refs):
        copies.append(pltpu.make_async_copy(ref, other_ref.at[pl.ds(place, ref.shape[0]), :], sems.at[i]))
        copies[-1].start()
        place += ref.shape[0]
    core = core_ref[0]

    def block_of(which, pieces, skip):
        group = group_ref[...]
        group_f = group.astype(F32)
        half_norms = 0.5 * jnp.sum(group_f * group_f, axis=1, keepdims=True)
        width = 2 * LANES
        rows = []
        start = skip
        for ref in pieces:
            for first in range(0, ref.shape[0], width):
                dots = lax.dot_general(
                    group, ref[pl.ds(first, width), :], (((1,), (1,)), ((), ())), preferred_element_type=F32
                )
                logits = (dots - half_norms) * scale
                logits_ref[which, :, pl.ds(start, width)] = logits
                top = jnp.max(logits, axis=0, keepdims=True)
                lse = top + jnp.log(jnp.sum(jnp.exp(logits - top), axis=0, keepdims=True))
                rows += [lse[:, i : i + LANES] for i in range(0, width, LANES)]
                start += width
        return jnp.concatenate(rows, axis=0)

    def spread(which, block):
        count = block.shape[0]
        place = pl.multiple_of((core if which == 0 else 1 - core) * count, count)
        for peer in range(part_ref.shape[0]):
            part_ref[peer, pl.ds(place, count), :] = block

    rows = other_ref.shape[0] // 2
    first, second = copies[: PIECES // 2], copies[PIECES // 2 :]

    @pl.when(core >= 0)
    def _():
        spread(0, block_of(0, own_refs, 0))

    for copy in first:
        copy.wait()

    @pl.when(core >= 0)
    def _():
        held_ref[...] = block_of(1, [other_ref.at[pl.ds(0, rows), :]], 0)

    for copy in second:
        copy.wait()

    @pl.when(core >= 0)
    def _():
        late = block_of(1, [other_ref.at[pl.ds(rows, rows), :]], rows)
        spread(1, jnp.concatenate([held_ref[...], late], axis=0))


def sums_kernel(core_ref, logits_ref, parts_ref, *refs):
    own_refs, (other_ref, send_ref, lse_ref, resp_ref, total_ref) = refs[:PIECES], refs[PIECES:]
    parts = parts_ref[...]
    top = jnp.max(parts, axis=0)
    total_ref[...] = top + jnp.log(jnp.sum(jnp.exp(parts - top[None]), axis=0))
    core = core_ref[0]
    points, width = other_ref.shape
    count = points // LANES
    mass = jnp.zeros((logits_ref.shape[1], LANES), F32)
    for which in range(CORES):
        place = pl.multiple_of((core if which == 0 else 1 - core) * count, count)
        lse = total_ref[pl.ds(place, count), :]
        if which == 0:
            lse_ref[...] = lse
        for i in range(count):
            cols = pl.ds(i * LANES, LANES)
            resp = jnp.exp(logits_ref[which, :, cols] - lse[i : i + 1, :]).astype(BF16)
            resp_ref[which, :, cols] = resp
            mass += resp.astype(F32)
    mass = jnp.sum(mass, axis=1, keepdims=True)
    high = mass.astype(BF16).astype(F32)
    lane = lax.broadcasted_iota(jnp.int32, (mass.shape[0], LANES), 1)
    send_ref[:, pl.ds(width, LANES)] = jnp.where(lane < LANES // 2, high, mass - high).astype(BF16)
    step = 2 * LANES
    for start in range(0, width, step):
        cols = pl.ds(start, step)
        sums = jnp.dot(resp_ref[1], other_ref[:, cols], preferred_element_type=F32)
        first = 0
        for ref in own_refs:
            part = pl.ds(first, ref.shape[0])
            sums += jnp.dot(resp_ref[0, :, part], ref[:, cols], preferred_element_type=F32)
            first += ref.shape[0]
        send_ref[:, cols] = sums.astype(BF16)


def update_kernel(got_ref, cent_ref, out_ref):
    own, width = cent_ref.shape
    step = 2 * own
    total = got_ref[pl.ds(0, step), :].astype(F32)
    for start in range(step, got_ref.shape[0], step):
        total += got_ref[pl.ds(start, step), :].astype(F32)
    total = total[:own] + total[own:]
    mass = total[:, width : width + 1] + total[:, width + LANES // 2 : width + LANES // 2 + 1]
    out_ref[...] = ((total[:, :width] + cent_ref[...].astype(F32)) / (mass + 1.0)).astype(BF16)


def body(points, centroids):
    rows, width = points.shape
    own = centroids.shape[0]
    chips = lax.axis_size("chip")
    groups = lax.axis_size("cent") * CORES
    rank = own * chips
    along = chips // ACROSS
    order = [[(x + y) % ACROSS * along + y for x in range(ACROSS) for y in range(along)]]
    params = pltpu.CompilerParams(vmem_limit_bytes=VMEM_LIMIT)
    smem = pl.BlockSpec(memory_space=pltpu.SMEM)
    core = lax.axis_index("core").astype(jnp.int32).reshape(1)

    sent = jnp.broadcast_to(centroids[None], (chips, own, width))
    sent, points = lax.optimization_barrier((sent, points))
    group = lax.all_to_all(sent, "chip", 0, 0, axis_index_groups=order).reshape(rank, width)

    mine = pl.pallas_call(
        stage_kernel,
        out_shape=[pltpu.VMEM((rows // PIECES, width), BF16)] * PIECES,
        in_specs=[pl.BlockSpec(memory_space=pl.ANY)],
        out_specs=whole(PIECES),
        scratch_shapes=[pltpu.SemaphoreType.DMA((PIECES,))],
        compiler_params=params,
        cost_estimate=pl.CostEstimate(flops=STAGE_FLOPS, transcendentals=0, bytes_accessed=4 * rows * width),
        name="stage",
    )(pltpu.with_memory_space_constraint(points, pltpu.HBM))
    mine = [in_vmem(x) for x in mine]
    theirs = [lax.ppermute(x, "core", [(0, 1), (1, 0)]) for x in mine]

    logits, part, other = pl.pallas_call(
        functools.partial(local_kernel, 2.0 / math.sqrt(width)),
        out_shape=(
            pltpu.VMEM((CORES, rank, rows), F32),
            jax.ShapeDtypeStruct((groups, CORES * rows // LANES, LANES), F32),
            pltpu.VMEM((rows, width), BF16),
        ),
        in_specs=[smem] + whole(1 + PIECES) + [pl.BlockSpec(memory_space=pl.ANY)] * PIECES,
        out_specs=tuple(whole(3)),
        scratch_shapes=[pltpu.VMEM((rows // 2 // LANES, LANES), F32), pltpu.SemaphoreType.DMA((PIECES,))],
        compiler_params=params,
        name="local",
    )(core, in_vmem(group), *mine, *theirs)

    parts = lax.all_to_all(part, ("core", "cent"), 0, 0)

    send, lse = pl.pallas_call(
        sums_kernel,
        out_shape=(
            jax.ShapeDtypeStruct((rank, width + LANES), BF16),
            jax.ShapeDtypeStruct((rows // LANES, LANES), F32),
        ),
        in_specs=[smem] + whole(3 + PIECES),
        out_specs=tuple(whole(2)),
        scratch_shapes=[
            pltpu.VMEM((CORES, rank, rows), BF16),
            pltpu.VMEM((CORES * rows // LANES, LANES), F32),
        ],
        compiler_params=params,
        name="sums",
    )(core, in_vmem(logits), in_vmem(parts), *mine, in_vmem(other))

    got = lax.all_to_all(send.reshape(chips, own, width + LANES), "chip", 0, 0, axis_index_groups=order)

    updated = pl.pallas_call(
        update_kernel,
        out_shape=jax.ShapeDtypeStruct((own, width), BF16),
        in_specs=whole(2),
        out_specs=whole(1)[0],
        compiler_params=params,
        name="update",
    )(in_vmem(got.reshape(rank, width + LANES)), centroids)
    return updated, lse.reshape(rows)


def solution(mesh):
    cent, pts = mesh.shape["cent"], mesh.shape["pts"]
    fine = Mesh(mesh.devices.reshape(cent, pts // CORES, CORES), ("cent", "chip", "core"))
    spread = P(("cent", "chip", "core"), None)
    return jax.shard_map(
        body,
        mesh=fine,
        in_specs=(P(("chip", "core"), None), spread),
        out_specs=(spread, P(("chip", "core"))),
        check_vma=False,
    )
```

time: 80.1 us -> 75.7 us (0.945)
  blocking collectives: 71.6 us -> 41.5 us
  starting transfers between devices: 1.92 us -> 18.9 us
  waiting for transfers between devices: 0.01 us -> 6.55 us
  Pallas kernels: 4.73 us -> 5.99 us
  local copies, waits for them, and re-layouts: 0.77 us -> 1.58 us
    all_to_all x3 -> x2, blocking collectives: 71.6 us -> 41.5 us  [the longest x1 22.8 us: body(): lax.all_to_all(send.reshape(chips, own, width + LANES), 'chip', 0, 0, axi...]
    all_to_all x0 -> x1, starting transfers between devices: none -> 10.2 us  [body(): lax.all_to_all(sent, 'chip', 0, 0, axis_index_groups=order)]
    ppermute x1 -> x4, starting transfers between devices: 1.92 us -> 8.66 us  [body(): theirs = [lax.ppermute(x, 'core', [(0, 1), (1, 0)]) for x in mine]]
    all_to_all x0 -> x1, waiting for transfers between devices: none -> 4.93 us  [body(): lax.all_to_all(sent, 'chip', 0, 0, axis_index_groups=order)]
    ppermute x1 -> x4, waiting for transfers between devices: 0.01 us -> 1.62 us  [body(): theirs = [lax.ppermute(x, 'core', [(0, 1), (1, 0)]) for x in mine]]
    pallas_call x0 -> x1, Pallas kernels: none -> 1.55 us  [body(): pl.pallas_call(stage_kernel, out_shape=[pltpu.VMEM((rows // PIECES, width...]
    broadcast_in_dim x1, local copies, waits for them, and re-layouts: 0.77 us -> 1.58 us  [body(): sent = jnp.broadcast_to(centroids[None], (chips, own, width))]
  transfers between devices with their start and end apart: 1 -> 5, of which waited for: 0 -> 2; matrix products, arithmetic and copies ran while one was open for 1% -> 0% of each run, Pallas kernels for 0% -> 2%
where the time goes in v3:
time: 75.7 us; the launch traced here: 75.2 us
  blocking collectives  41.5 us (55%)
  starting transfers between devices  18.9 us (25%)
  waiting for transfers between devices  6.55 us (9%)
  Pallas kernels  5.99 us (8%)
  local copies, waits for them, and re-layouts  1.58 us (2%)
    all_to_all x1, blocking collectives, body(): lax.all_to_all(send.reshape(chips, own, width + LANES), 'chip', 0, 0, axi...  22.8 us
    all_to_all x1, blocking collectives, body(): parts = lax.all_to_all(part, ('core', 'cent'), 0, 0)  18.7 us
    all_to_all x1, starting transfers between devices, body(): lax.all_to_all(sent, 'chip', 0, 0, axis_index_groups=order)  10.2 us
    ppermute x4, starting transfers between devices, body(): theirs = [lax.ppermute(x, 'core', [(0, 1), (1, 0)]) for x in mine]  8.66 us
    all_to_all x1, waiting for transfers between devices, body(): lax.all_to_all(sent, 'chip', 0, 0, axis_index_groups=order)  4.93 us
    pallas_call x1, Pallas kernels, body(): pl.pallas_call(functools.partial(local_kernel, 2.0 / math.sqrt(width)), o...  2.3 us
    ppermute x4, waiting for transfers between devices, body(): theirs = [lax.ppermute(x, 'core', [(0, 1), (1, 0)]) for x in mine]  1.62 us
    broadcast_in_dim x1, local copies, waits for them, and re-layouts, body(): sent = jnp.broadcast_to(centroids[None], (chips, own, width))  1.58 us
  transfers between devices with their start and end apart: 5, of which 2 were waited for; matrix products, arithmetic and copies ran while one was open for 0% of the time, Pallas kernels for 2%

profile of v3, /device:TPU:8, one launch (start us, length us, event | category | flops | bytes accessed | tf_op | source)
XLA Modules:
  0.0 75.2 jit_solution(7514240559438757233)
XLA Ops:
  0.6 1.6 %broadcast_in_dim.2 = bf16[32,8,1024]{2,1,0:T(8,128)(2,1)} broadcast(bf16[8,1024]{1,0:T(8,128)(2,1)} %cent_ref.1), dimensions={1,2} | broadcast | bytes 540672 | tf_op jit(solution)/shard_map/broadcast_in_dim | solution.py:157
  2.2 10.2 %all-to-all-start = ((bf16[32,8,1024]{2,1,0:T(8,128)(2,1)}), bf16[32,8,1024]{2,1,0:T(8,128)(2,1)S(1)}, u32[]{:S(2)}, u32[]{:S(2)}) async-start(bf16[32,8,1024]{2,1,0:T(8,128)(2,1)} %broadcast_in_dim.2), calls=%async_computation | async-start | bytes 1048576 | tf_op jit(solution)/shard_map/all_to_all | solution.py:159
  12.4 1.6 %stage.1 = (bf16[256,1024]{1,0:T(8,128)(2,1)S(1)}, bf16[256,1024]{1,0:T(8,128)(2,1)S(1)}, bf16[256,1024]{1,0:T(8,128)(2,1)S(1)}, bf16[256,1024]{1,0:T(8,128)(2,1)S(1)}) custom-call(bf16[1024,1024]{1,0:T(8,128)(2,1)} %points_ref), custom_call_target="tpu_custom_call" | custom-call | flops 10000000000 | bytes 4194304 | tf_op jit(solution)/shard_map/stage/pallas_call | solution.py:161
  14.0 1.9 %collective-permute-start = (bf16[256,1024]{1,0:T(8,128)(2,1)S(1)}, bf16[256,1024]{1,0:T(8,128)(2,1)S(1)}, u32[]{:S(2)}, u32[]{:S(2)}) collective-permute-start(bf16[256,1024]{1,0:T(8,128)(2,1)S(1)} %get-tuple-element.15.refs_0_), channel_id=1, source_target_pairs={{0,1},{1,0},{2,3},{3,2},{4,5},{5,4},{6,7},{7,6},{8,9},{9,8},{10,11... | collective-permute-start | bytes 1572872 | tf_op jit(solution)/shard_map/ppermute | solution.py:172
  15.9 2.4 %collective-permute-start.1 = (bf16[256,1024]{1,0:T(8,128)(2,1)S(1)}, bf16[256,1024]{1,0:T(8,128)(2,1)}, u32[]{:S(2)}, u32[]{:S(2)}) collective-permute-start(bf16[256,1024]{1,0:T(8,128)(2,1)S(1)} %get-tuple-element.16.refs_1_), channel_id=1, source_target_pairs={{0,1},{1,0},{2,3},{3,2},{4,5},{5,4},{6,7},{7,6},{8,9},{9,8},{10,11... | collective-permute-start | bytes 1572872 | tf_op jit(solution)/shard_map/ppermute | solution.py:172
  18.3 1.9 %collective-permute-start.2 = (bf16[256,1024]{1,0:T(8,128)(2,1)S(1)}, bf16[256,1024]{1,0:T(8,128)(2,1)}, u32[]{:S(2)}, u32[]{:S(2)}) collective-permute-start(bf16[256,1024]{1,0:T(8,128)(2,1)S(1)} %get-tuple-element.17.refs_2_), channel_id=1, source_target_pairs={{0,1},{1,0},{2,3},{3,2},{4,5},{5,4},{6,7},{7,6},{8,9},{9,8},{10,11... | collective-permute-start | bytes 1572872 | tf_op jit(solution)/shard_map/ppermute | solution.py:172
  20.3 2.4 %collective-permute-start.3 = (bf16[256,1024]{1,0:T(8,128)(2,1)S(1)}, bf16[256,1024]{1,0:T(8,128)(2,1)}, u32[]{:S(2)}, u32[]{:S(2)}) collective-permute-start(bf16[256,1024]{1,0:T(8,128)(2,1)S(1)} %get-tuple-element.18.refs_3_), channel_id=1, source_target_pairs={{0,1},{1,0},{2,3},{3,2},{4,5},{5,4},{6,7},{7,6},{8,9},{9,8},{10,11... | collective-permute-start | bytes 1572872 | tf_op jit(solution)/shard_map/ppermute | solution.py:172
  22.7 0.0 collective-permute-done.refs_4_
  22.7 0.0 collective-permute-done.1.refs_5_
  22.7 0.0 collective-permute-done.2.refs_6_
  22.7 1.6 %collective-permute-done.3.refs_7_ = bf16[256,1024]{1,0:T(8,128)(2,1)} collective-permute-done((bf16[256,1024]{1,0:T(8,128)(2,1)S(1)}, bf16[256,1024]{1,0:T(8,128)(2,1)}, u32[]{:S(2)}, u32[]{:S(2)}) %collective-permute-start.3) | collective-permute-done | bytes 524320 | tf_op jit(solution)/shard_map/ppermute | solution.py:172
  24.3 4.9 %all-to-all-done = bf16[32,8,1024]{2,1,0:T(8,128)(2,1)S(1)} async-done(((bf16[32,8,1024]{2,1,0:T(8,128)(2,1)}), bf16[32,8,1024]{2,1,0:T(8,128)(2,1)S(1)}, u32[]{:S(2)}, u32[]{:S(2)}) %all-to-all-start) | async-done | bytes 524320 | tf_op jit(solution)/shard_map/all_to_all | solution.py:159
  29.3 2.3 %local.1 = (f32[2,256,1024]{2,1,0:T(8,128)S(1)}, f32[16,16,128]{2,1,0:T(8,128)S(1)}, bf16[1024,1024]{1,0:T(8,128)(2,1)S(1)}) custom-call(s32[1]{0:T(128)} %bitcast.core_ref, bf16[256,1024]{1,0:T(8,128)(2,1)S(1)} %bitcast.6, bf16[256,1024]{1,0:T(8,128)(2,1)S(1)} %get-tuple-element.15.refs_0_, bf16[256,1024]{1,0:T(8,128)(2,1)S(1)} %get-tuple-element.16.refs_1_, ...), custom_call_target="tpu_custom_call" | custom-call | tf_op jit(solution)/shard_map/local/pallas_call | solution.py:174
  31.6 18.7 %all_to_all.15.parts_ref = f32[16,16,128]{2,1,0:T(8,128)S(1)} all-to-all(f32[16,16,128]{2,1,0:T(8,128)S(1)} %get-tuple-element.20), channel_id=1, replica_groups=mesh['cent'=8,'chip'=32,'core'=2] {'core','cent'}, dimensions={0} | all-to-all | bytes 262144 | tf_op jit(solution)/shard_map/all_to_all | solution.py:188
  50.3 0.0 copy-start
  50.3 1.4 %sums.1 = (bf16[256,1152]{1,0:T(8,128)(2,1)S(1)}, f32[8,128]{1,0:T(8,128)}) custom-call(s32[1]{0:T(128)} %bitcast.core_ref, f32[2,256,1024]{2,1,0:T(8,128)S(1)} %get-tuple-element.19.logits_ref, f32[16,16,128]{2,1,0:T(8,128)S(1)} %all_to_all.15.parts_ref, bf16[256,1024]{1,0:T(8,128)(2,1)S(1)} %get-tuple-element.15.refs_0_, ...), custom_call_target="tpu_custom_call" | custom-call | tf_op jit(solution)/shard_map/sums/pallas_call | solution.py:190
  51.6 22.8 %all_to_all.16 = bf16[32,8,1152]{2,1,0:T(8,128)(2,1)S(1)} all-to-all(bf16[32,8,1152]{2,1,0:T(8,128)(2,1)S(1)} %bitcast.7), channel_id=1, replica_groups={{0,18,36,54,8,26,44,62,16,34,52,6,24,42,60,14,32,50,4,22,40,58,12,30,48..., dimensions={0} | all-to-all | bytes 1179648 | tf_op jit(solution)/shard_map/all_to_all | solution.py:206
  74.5 0.0 copy-done
  74.5 0.8 %update.1 = bf16[8,1024]{1,0:T(8,128)(2,1)} custom-call(bf16[256,1152]{1,0:T(8,128)(2,1)S(1)} %bitcast.5, bf16[8,1024]{1,0:T(8,128)(2,1)S(1)} %copy-done), custom_call_target="tpu_custom_call" | custom-call | tf_op jit(solution)/shard_map/update/pallas_call | solution.py:208
Async XLA Ops:
  2.2 27.1 %all-to-all-start = ((bf16[32,8,1024]{2,1,0:T(8,128)(2,1)}), bf16[32,8,1024]{2,1,0:T(8,128)(2,1)S(1)}, u32[]{:S(2)}, u32[]{:S(2)}) async-start(bf16[32,8,1024]{2,1,0:T(8,128)(2,1)} %broadcast_in_dim.2), calls=%async_computation | async-start | bytes 1048576 | tf_op jit(solution)/shard_map/all_to_all | solution.py:159
  14.0 8.7 %collective-permute-start = (bf16[256,1024]{1,0:T(8,128)(2,1)S(1)}, bf16[256,1024]{1,0:T(8,128)(2,1)S(1)}, u32[]{:S(2)}, u32[]{:S(2)}) collective-permute-start(bf16[256,1024]{1,0:T(8,128)(2,1)S(1)} %get-tuple-element.15.refs_0_), channel_id=1, source_target_pairs={{0,1},{1,0},{2,3},{3,2},{4,5},{5,4},{6,7},{7,6},{8,9},{9,8},{10,11... | collective-permute-start | bytes 1572872 | tf_op jit(solution)/shard_map/ppermute | solution.py:172
  15.9 6.8 %collective-permute-start.1 = (bf16[256,1024]{1,0:T(8,128)(2,1)S(1)}, bf16[256,1024]{1,0:T(8,128)(2,1)}, u32[]{:S(2)}, u32[]{:S(2)}) collective-permute-start(bf16[256,1024]{1,0:T(8,128)(2,1)S(1)} %get-tuple-element.16.refs_1_), channel_id=1, source_target_pairs={{0,1},{1,0},{2,3},{3,2},{4,5},{5,4},{6,7},{7,6},{8,9},{9,8},{10,11... | collective-permute-start | bytes 1572872 | tf_op jit(solution)/shard_map/ppermute | solution.py:172
  18.3 4.4 %collective-permute-start.2 = (bf16[256,1024]{1,0:T(8,128)(2,1)S(1)}, bf16[256,1024]{1,0:T(8,128)(2,1)}, u32[]{:S(2)}, u32[]{:S(2)}) collective-permute-start(bf16[256,1024]{1,0:T(8,128)(2,1)S(1)} %get-tuple-element.17.refs_2_), channel_id=1, source_target_pairs={{0,1},{1,0},{2,3},{3,2},{4,5},{5,4},{6,7},{7,6},{8,9},{9,8},{10,11... | collective-permute-start | bytes 1572872 | tf_op jit(solution)/shard_map/ppermute | solution.py:172
  20.3 4.1 %collective-permute-start.3 = (bf16[256,1024]{1,0:T(8,128)(2,1)S(1)}, bf16[256,1024]{1,0:T(8,128)(2,1)}, u32[]{:S(2)}, u32[]{:S(2)}) collective-permute-start(bf16[256,1024]{1,0:T(8,128)(2,1)S(1)} %get-tuple-element.18.refs_3_), channel_id=1, source_target_pairs={{0,1},{1,0},{2,3},{3,2},{4,5},{5,4},{6,7},{7,6},{8,9},{9,8},{10,11... | collective-permute-start | bytes 1572872 | tf_op jit(solution)/shard_map/ppermute | solution.py:172
  50.3 24.2 %copy-start = (bf16[8,1024]{1,0:T(8,128)(2,1)S(1)}, bf16[8,1024]{1,0:T(8,128)(2,1)}, u32[]{:S(2)}) copy-start(bf16[8,1024]{1,0:T(8,128)(2,1)} %cent_ref.1) | copy-start | bytes 49156

commit v4 on v3

--- a/solution.py
+++ b/solution.py
@@ -149,14 +149,15 @@
     groups = lax.axis_size("cent") * CORES
     rank = own * chips
     along = chips // ACROSS
-    order = [[(x + y) % ACROSS * along + y for x in range(ACROSS) for y in range(along)]]
+    line = [x * along + (y + 2 * x) % along for y in range(along) for x in range(ACROSS)]
+    order = [[CORES * k for k in line], [CORES * k + 1 for k in reversed(line)]]
     params = pltpu.CompilerParams(vmem_limit_bytes=VMEM_LIMIT)
     smem = pl.BlockSpec(memory_space=pltpu.SMEM)
     core = lax.axis_index("core").astype(jnp.int32).reshape(1)
 
     sent = jnp.broadcast_to(centroids[None], (chips, own, width))
     sent, points = lax.optimization_barrier((sent, points))
-    group = lax.all_to_all(sent, "chip", 0, 0, axis_index_groups=order).reshape(rank, width)
+    group = lax.all_to_all(sent, ("chip", "core"), 0, 0, axis_index_groups=order).reshape(rank, width)
 
     mine = pl.pallas_call(
         stage_kernel,
@@ -203,7 +204,7 @@
         name="sums",
     )(core, in_vmem(logits), in_vmem(parts), *mine, in_vmem(other))
 
-    got = lax.all_to_all(send.reshape(chips, own, width + LANES), "chip", 0, 0, axis_index_groups=order)
+    got = lax.all_to_all(send.reshape(chips, own, width + LANES), ("chip", "core"), 0, 0, axis_index_groups=order)
 
     updated = pl.pallas_call(
         update_kernel,

time: 75.7 us -> 72 us (0.951)
  the two profiles are of different devices: /device:TPU:8 before, /device:TPU:6 now
where the time goes in v4:
time: 72 us; the launch traced here: 71.5 us
  blocking collectives  41.1 us (57%)
  starting transfers between devices  18.9 us (26%)
  Pallas kernels  5.99 us (8%)
  waiting for transfers between devices  3.26 us (5%)
  local copies, waits for them, and re-layouts  1.58 us (2%)
  between operations  0.72 us (1%)
    all_to_all x1, blocking collectives, body(): lax.all_to_all(send.reshape(chips, own, width + LANES), ('chip', 'core'),...  22.4 us
    all_to_all x1, blocking collectives, body(): parts = lax.all_to_all(part, ('core', 'cent'), 0, 0)  18.7 us
    all_to_all x1, starting transfers between devices, body(): lax.all_to_all(sent, ('chip', 'core'), 0, 0, axis_index_groups=order)  10.2 us
    ppermute x4, starting transfers between devices, body(): theirs = [lax.ppermute(x, 'core', [(0, 1), (1, 0)]) for x in mine]  8.66 us
    pallas_call x1, Pallas kernels, body(): pl.pallas_call(functools.partial(local_kernel, 2.0 / math.sqrt(width)), o...  2.3 us
    all_to_all x1, waiting for transfers between devices, body(): lax.all_to_all(sent, ('chip', 'core'), 0, 0, axis_index_groups=order)  1.64 us
    ppermute x4, waiting for transfers between devices, body(): theirs = [lax.ppermute(x, 'core', [(0, 1), (1, 0)]) for x in mine]  1.62 us
    broadcast_in_dim x1, local copies, waits for them, and re-layouts, body(): sent = jnp.broadcast_to(centroids[None], (chips, own, width))  1.58 us
  transfers between devices with their start and end apart: 5, of which 2 were waited for; matrix products, arithmetic and copies ran while one was open for 0% of the time, Pallas kernels for 2%

profile of v4, /device:TPU:6, one launch (start us, length us, event | category | flops | bytes accessed | tf_op | source)
XLA Modules:
  0.0 71.5 jit_solution(5840615699782217277)
XLA Ops:
  0.6 1.6 %broadcast_in_dim.2 = bf16[32,8,1024]{2,1,0:T(8,128)(2,1)} broadcast(bf16[8,1024]{1,0:T(8,128)(2,1)} %cent_ref.1), dimensions={1,2} | broadcast | bytes 540672 | tf_op jit(solution)/shard_map/broadcast_in_dim | solution.py:158
  2.2 10.2 %all-to-all-start = ((bf16[32,8,1024]{2,1,0:T(8,128)(2,1)}), bf16[32,8,1024]{2,1,0:T(8,128)(2,1)S(1)}, u32[]{:S(2)}, u32[]{:S(2)}) async-start(bf16[32,8,1024]{2,1,0:T(8,128)(2,1)} %broadcast_in_dim.2), calls=%async_computation | async-start | bytes 1048576 | tf_op jit(solution)/shard_map/all_to_all | solution.py:160
  12.4 1.6 %stage.1 = (bf16[256,1024]{1,0:T(8,128)(2,1)S(1)}, bf16[256,1024]{1,0:T(8,128)(2,1)S(1)}, bf16[256,1024]{1,0:T(8,128)(2,1)S(1)}, bf16[256,1024]{1,0:T(8,128)(2,1)S(1)}) custom-call(bf16[1024,1024]{1,0:T(8,128)(2,1)} %points_ref), custom_call_target="tpu_custom_call" | custom-call | flops 10000000000 | bytes 4194304 | tf_op jit(solution)/shard_map/stage/pallas_call | solution.py:162
  14.0 1.9 %collective-permute-start = (bf16[256,1024]{1,0:T(8,128)(2,1)S(1)}, bf16[256,1024]{1,0:T(8,128)(2,1)S(1)}, u32[]{:S(2)}, u32[]{:S(2)}) collective-permute-start(bf16[256,1024]{1,0:T(8,128)(2,1)S(1)} %get-tuple-element.15.refs_0_), channel_id=1, source_target_pairs={{0,1},{1,0},{2,3},{3,2},{4,5},{5,4},{6,7},{7,6},{8,9},{9,8},{10,11... | collective-permute-start | bytes 1572872 | tf_op jit(solution)/shard_map/ppermute | solution.py:173
  15.9 2.4 %collective-permute-start.1 = (bf16[256,1024]{1,0:T(8,128)(2,1)S(1)}, bf16[256,1024]{1,0:T(8,128)(2,1)}, u32[]{:S(2)}, u32[]{:S(2)}) collective-permute-start(bf16[256,1024]{1,0:T(8,128)(2,1)S(1)} %get-tuple-element.16.refs_1_), channel_id=1, source_target_pairs={{0,1},{1,0},{2,3},{3,2},{4,5},{5,4},{6,7},{7,6},{8,9},{9,8},{10,11... | collective-permute-start | bytes 1572872 | tf_op jit(solution)/shard_map/ppermute | solution.py:173
  18.3 1.9 %collective-permute-start.2 = (bf16[256,1024]{1,0:T(8,128)(2,1)S(1)}, bf16[256,1024]{1,0:T(8,128)(2,1)}, u32[]{:S(2)}, u32[]{:S(2)}) collective-permute-start(bf16[256,1024]{1,0:T(8,128)(2,1)S(1)} %get-tuple-element.17.refs_2_), channel_id=1, source_target_pairs={{0,1},{1,0},{2,3},{3,2},{4,5},{5,4},{6,7},{7,6},{8,9},{9,8},{10,11... | collective-permute-start | bytes 1572872 | tf_op jit(solution)/shard_map/ppermute | solution.py:173
  20.2 2.4 %collective-permute-start.3 = (bf16[256,1024]{1,0:T(8,128)(2,1)S(1)}, bf16[256,1024]{1,0:T(8,128)(2,1)}, u32[]{:S(2)}, u32[]{:S(2)}) collective-permute-start(bf16[256,1024]{1,0:T(8,128)(2,1)S(1)} %get-tuple-element.18.refs_3_), channel_id=1, source_target_pairs={{0,1},{1,0},{2,3},{3,2},{4,5},{5,4},{6,7},{7,6},{8,9},{9,8},{10,11... | collective-permute-start | bytes 1572872 | tf_op jit(solution)/shard_map/ppermute | solution.py:173
  22.7 0.0 collective-permute-done.refs_4_
  22.7 0.0 collective-permute-done.1.refs_5_
  22.7 0.0 collective-permute-done.2.refs_6_
  22.7 1.6 %collective-permute-done.3.refs_7_ = bf16[256,1024]{1,0:T(8,128)(2,1)} collective-permute-done((bf16[256,1024]{1,0:T(8,128)(2,1)S(1)}, bf16[256,1024]{1,0:T(8,128)(2,1)}, u32[]{:S(2)}, u32[]{:S(2)}) %collective-permute-start.3) | collective-permute-done | bytes 524320 | tf_op jit(solution)/shard_map/ppermute | solution.py:173
  24.3 1.6 %all-to-all-done = bf16[32,8,1024]{2,1,0:T(8,128)(2,1)S(1)} async-done(((bf16[32,8,1024]{2,1,0:T(8,128)(2,1)}), bf16[32,8,1024]{2,1,0:T(8,128)(2,1)S(1)}, u32[]{:S(2)}, u32[]{:S(2)}) %all-to-all-start) | async-done | bytes 524320 | tf_op jit(solution)/shard_map/all_to_all | solution.py:160
  25.9 2.3 %local.1 = (f32[2,256,1024]{2,1,0:T(8,128)S(1)}, f32[16,16,128]{2,1,0:T(8,128)S(1)}, bf16[1024,1024]{1,0:T(8,128)(2,1)S(1)}) custom-call(s32[1]{0:T(128)} %bitcast.core_ref, bf16[256,1024]{1,0:T(8,128)(2,1)S(1)} %bitcast.6, bf16[256,1024]{1,0:T(8,128)(2,1)S(1)} %get-tuple-element.15.refs_0_, bf16[256,1024]{1,0:T(8,128)(2,1)S(1)} %get-tuple-element.16.refs_1_, ...), custom_call_target="tpu_custom_call" | custom-call | tf_op jit(solution)/shard_map/local/pallas_call | solution.py:175
  28.3 18.7 %all_to_all.15.parts_ref = f32[16,16,128]{2,1,0:T(8,128)S(1)} all-to-all(f32[16,16,128]{2,1,0:T(8,128)S(1)} %get-tuple-element.20), channel_id=1, replica_groups=mesh['cent'=8,'chip'=32,'core'=2] {'core','cent'}, dimensions={0} | all-to-all | bytes 262144 | tf_op jit(solution)/shard_map/all_to_all | solution.py:189
  46.9 0.0 copy-start
  47.0 1.4 %sums.1 = (bf16[256,1152]{1,0:T(8,128)(2,1)S(1)}, f32[8,128]{1,0:T(8,128)}) custom-call(s32[1]{0:T(128)} %bitcast.core_ref, f32[2,256,1024]{2,1,0:T(8,128)S(1)} %get-tuple-element.19.logits_ref, f32[16,16,128]{2,1,0:T(8,128)S(1)} %all_to_all.15.parts_ref, bf16[256,1024]{1,0:T(8,128)(2,1)S(1)} %get-tuple-element.15.refs_0_, ...), custom_call_target="tpu_custom_call" | custom-call | tf_op jit(solution)/shard_map/sums/pallas_call | solution.py:191
  48.3 22.4 %all_to_all.16 = bf16[32,8,1152]{2,1,0:T(8,128)(2,1)S(1)} all-to-all(bf16[32,8,1152]{2,1,0:T(8,128)(2,1)S(1)} %bitcast.7), channel_id=1, replica_groups={{0,20,40,60,2,22,42,62,4,24,44,48,6,26,46,50,8,28,32,52,10,30,34,54,12,..., dimensions={0} | all-to-all | bytes 1179648 | tf_op jit(solution)/shard_map/all_to_all | solution.py:207
  70.7 0.0 copy-done
  70.7 0.8 %update.1 = bf16[8,1024]{1,0:T(8,128)(2,1)} custom-call(bf16[256,1152]{1,0:T(8,128)(2,1)S(1)} %bitcast.5, bf16[8,1024]{1,0:T(8,128)(2,1)S(1)} %copy-done), custom_call_target="tpu_custom_call" | custom-call | tf_op jit(solution)/shard_map/update/pallas_call | solution.py:209
Async XLA Ops:
  2.2 23.7 %all-to-all-start = ((bf16[32,8,1024]{2,1,0:T(8,128)(2,1)}), bf16[32,8,1024]{2,1,0:T(8,128)(2,1)S(1)}, u32[]{:S(2)}, u32[]{:S(2)}) async-start(bf16[32,8,1024]{2,1,0:T(8,128)(2,1)} %broadcast_in_dim.2), calls=%async_computation | async-start | bytes 1048576 | tf_op jit(solution)/shard_map/all_to_all | solution.py:160
  14.0 8.7 %collective-permute-start = (bf16[256,1024]{1,0:T(8,128)(2,1)S(1)}, bf16[256,1024]{1,0:T(8,128)(2,1)S(1)}, u32[]{:S(2)}, u32[]{:S(2)}) collective-permute-start(bf16[256,1024]{1,0:T(8,128)(2,1)S(1)} %get-tuple-element.15.refs_0_), channel_id=1, source_target_pairs={{0,1},{1,0},{2,3},{3,2},{4,5},{5,4},{6,7},{7,6},{8,9},{9,8},{10,11... | collective-permute-start | bytes 1572872 | tf_op jit(solution)/shard_map/ppermute | solution.py:173
  15.9 6.8 %collective-permute-start.1 = (bf16[256,1024]{1,0:T(8,128)(2,1)S(1)}, bf16[256,1024]{1,0:T(8,128)(2,1)}, u32[]{:S(2)}, u32[]{:S(2)}) collective-permute-start(bf16[256,1024]{1,0:T(8,128)(2,1)S(1)} %get-tuple-element.16.refs_1_), channel_id=1, source_target_pairs={{0,1},{1,0},{2,3},{3,2},{4,5},{5,4},{6,7},{7,6},{8,9},{9,8},{10,11... | collective-permute-start | bytes 1572872 | tf_op jit(solution)/shard_map/ppermute | solution.py:173
  18.3 4.4 %collective-permute-start.2 = (bf16[256,1024]{1,0:T(8,128)(2,1)S(1)}, bf16[256,1024]{1,0:T(8,128)(2,1)}, u32[]{:S(2)}, u32[]{:S(2)}) collective-permute-start(bf16[256,1024]{1,0:T(8,128)(2,1)S(1)} %get-tuple-element.17.refs_2_), channel_id=1, source_target_pairs={{0,1},{1,0},{2,3},{3,2},{4,5},{5,4},{6,7},{7,6},{8,9},{9,8},{10,11... | collective-permute-start | bytes 1572872 | tf_op jit(solution)/shard_map/ppermute | solution.py:173
  20.2 4.1 %collective-permute-start.3 = (bf16[256,1024]{1,0:T(8,128)(2,1)S(1)}, bf16[256,1024]{1,0:T(8,128)(2,1)}, u32[]{:S(2)}, u32[]{:S(2)}) collective-permute-start(bf16[256,1024]{1,0:T(8,128)(2,1)S(1)} %get-tuple-element.18.refs_3_), channel_id=1, source_target_pairs={{0,1},{1,0},{2,3},{3,2},{4,5},{5,4},{6,7},{7,6},{8,9},{9,8},{10,11... | collective-permute-start | bytes 1572872 | tf_op jit(solution)/shard_map/ppermute | solution.py:173
  46.9 23.8 %copy-start = (bf16[8,1024]{1,0:T(8,128)(2,1)S(1)}, bf16[8,1024]{1,0:T(8,128)(2,1)}, u32[]{:S(2)}) copy-start(bf16[8,1024]{1,0:T(8,128)(2,1)} %cent_ref.1) | copy-start | bytes 49156

commit v5 on v4

--- a/solution.py
+++ b/solution.py
@@ -38,7 +38,7 @@
 
 
 def local_kernel(scale, core_ref, group_ref, *refs):
-    own_refs, from_refs = refs[:PIECES], refs[PIECES : 2 * PIECES]
+    own_refs, near_ref, from_refs = refs[:PIECES], refs[PIECES], refs[PIECES + 1 : 2 * PIECES]
     logits_ref, part_ref, other_ref, held_ref, sems = refs[2 * PIECES :]
     copies, place = [], 0
     for i, ref in enumerate(from_refs):
@@ -73,36 +73,28 @@
         for peer in range(part_ref.shape[0]):
             part_ref[peer, pl.ds(place, count), :] = block
 
-    rows = other_ref.shape[0] // 2
-    first, second = copies[: PIECES // 2], copies[PIECES // 2 :]
-
     @pl.when(core >= 0)
     def _():
         spread(0, block_of(0, own_refs, 0))
-
-    for copy in first:
+        held_ref[...] = block_of(1, [near_ref], other_ref.shape[0])
+
+    for copy in copies:
         copy.wait()
 
     @pl.when(core >= 0)
     def _():
-        held_ref[...] = block_of(1, [other_ref.at[pl.ds(0, rows), :]], 0)
-
-    for copy in second:
-        copy.wait()
-
-    @pl.when(core >= 0)
-    def _():
-        late = block_of(1, [other_ref.at[pl.ds(rows, rows), :]], rows)
-        spread(1, jnp.concatenate([held_ref[...], late], axis=0))
+        spread(1, jnp.concatenate([block_of(1, [other_ref], 0), held_ref[...]], axis=0))
 
 
 def sums_kernel(core_ref, logits_ref, parts_ref, *refs):
-    own_refs, (other_ref, send_ref, lse_ref, resp_ref, total_ref) = refs[:PIECES], refs[PIECES:]
+    own_refs, near_ref = refs[:PIECES], refs[PIECES]
+    other_ref, send_ref, lse_ref, resp_ref, total_ref = refs[PIECES + 1 :]
     parts = parts_ref[...]
     top = jnp.max(parts, axis=0)
     total_ref[...] = top + jnp.log(jnp.sum(jnp.exp(parts - top[None]), axis=0))
     core = core_ref[0]
-    points, width = other_ref.shape
+    points, width = resp_ref.shape[2], other_ref.shape[1]
+    far = other_ref.shape[0]
     count = points // LANES
     mass = jnp.zeros((logits_ref.shape[1], LANES), F32)
     for which in range(CORES):
@@ -122,7 +114,8 @@
     step = 2 * LANES
     for start in range(0, width, step):
         cols = pl.ds(start, step)
-        sums = jnp.dot(resp_ref[1], other_ref[:, cols], preferred_element_type=F32)
+        sums = jnp.dot(resp_ref[1, :, pl.ds(0, far)], other_ref[:, cols], preferred_element_type=F32)
+        sums += jnp.dot(resp_ref[1, :, pl.ds(far, points - far)], near_ref[:, cols], preferred_element_type=F32)
         first = 0
         for ref in own_refs:
             part = pl.ds(first, ref.shape[0])
@@ -172,19 +165,22 @@
     mine = [in_vmem(x) for x in mine]
     theirs = [lax.ppermute(x, "core", [(0, 1), (1, 0)]) for x in mine]
 
+    *theirs, near = theirs
+    near = in_vmem(near)
+
     logits, part, other = pl.pallas_call(
         functools.partial(local_kernel, 2.0 / math.sqrt(width)),
         out_shape=(
             pltpu.VMEM((CORES, rank, rows), F32),
             jax.ShapeDtypeStruct((groups, CORES * rows // LANES, LANES), F32),
-            pltpu.VMEM((rows, width), BF16),
+            pltpu.VMEM((rows - rows // PIECES, width), BF16),
         ),
-        in_specs=[smem] + whole(1 + PIECES) + [pl.BlockSpec(memory_space=pl.ANY)] * PIECES,
+        in_specs=[smem] + whole(2 + PIECES) + [pl.BlockSpec(memory_space=pl.ANY)] * (PIECES - 1),
         out_specs=tuple(whole(3)),
-        scratch_shapes=[pltpu.VMEM((rows // 2 // LANES, LANES), F32), pltpu.SemaphoreType.DMA((PIECES,))],
+        scratch_shapes=[pltpu.VMEM((rows // PIECES // LANES, LANES), F32), pltpu.SemaphoreType.DMA((PIECES - 1,))],
         compiler_params=params,
         name="local",
-    )(core, in_vmem(group), *mine, *theirs)
+    )(core, in_vmem(group), *mine, near, *theirs)
 
     parts = lax.all_to_all(part, ("core", "cent"), 0, 0)
 
@@ -194,7 +190,7 @@
             jax.ShapeDtypeStruct((rank, width + LANES), BF16),
             jax.ShapeDtypeStruct((rows // LANES, LANES), F32),
         ),
-        in_specs=[smem] + whole(3 + PIECES),
+        in_specs=[smem] + whole(4 + PIECES),
         out_specs=tuple(whole(2)),
         scratch_shapes=[
             pltpu.VMEM((CORES, rank, rows), BF16),
@@ -202,7 +198,7 @@
         ],
         compiler_params=params,
         name="sums",
-    )(core, in_vmem(logits), in_vmem(parts), *mine, in_vmem(other))
+    )(core, in_vmem(logits), in_vmem(parts), *mine, near, in_vmem(other))
 
     got = lax.all_to_all(send.reshape(chips, own, width + LANES), ("chip", "core"), 0, 0, axis_index_groups=order)
 

time: 72 us -> 71.8 us (level)
  no operation moved by 1% of the time
where the time goes in v5:
time: 71.8 us; the launch traced here: 71.3 us
  blocking collectives  41 us (57%)
  starting transfers between devices  18.9 us (26%)
  Pallas kernels  5.83 us (8%)
  waiting for transfers between devices  3.26 us (5%)
  local copies, waits for them, and re-layouts  1.58 us (2%)
  between operations  0.72 us (1%)
    all_to_all x1, blocking collectives, body(): lax.all_to_all(send.reshape(chips, own, width + LANES), ('chip', 'core'),...  22.4 us
    all_to_all x1, blocking collectives, body(): parts = lax.all_to_all(part, ('core', 'cent'), 0, 0)  18.7 us
    all_to_all x1, starting transfers between devices, body(): lax.all_to_all(sent, ('chip', 'core'), 0, 0, axis_index_groups=order)  10.2 us
    ppermute x4, starting transfers between devices, body(): theirs = [lax.ppermute(x, 'core', [(0, 1), (1, 0)]) for x in mine]  8.66 us
    pallas_call x1, Pallas kernels, body(): pl.pallas_call(functools.partial(local_kernel, 2.0 / math.sqrt(width)), o...  2.14 us
    all_to_all x1, waiting for transfers between devices, body(): lax.all_to_all(sent, ('chip', 'core'), 0, 0, axis_index_groups=order)  1.77 us
    broadcast_in_dim x1, local copies, waits for them, and re-layouts, body(): sent = jnp.broadcast_to(centroids[None], (chips, own, width))  1.58 us
    pallas_call x1, Pallas kernels, body(): pl.pallas_call(stage_kernel, out_shape=[pltpu.VMEM((rows // PIECES, width...  1.55 us
  transfers between devices with their start and end apart: 5, of which 2 were waited for; matrix products, arithmetic and copies ran while one was open for 0% of the time, Pallas kernels for 2%

profile of v5, /device:TPU:6, one launch (start us, length us, event | category | flops | bytes accessed | tf_op | source)
XLA Modules:
  0.0 71.3 jit_solution(4882696379894110529)
XLA Ops:
  0.6 1.6 %broadcast_in_dim.2 = bf16[32,8,1024]{2,1,0:T(8,128)(2,1)} broadcast(bf16[8,1024]{1,0:T(8,128)(2,1)} %cent_ref.1), dimensions={1,2} | broadcast | bytes 540672 | tf_op jit(solution)/shard_map/broadcast_in_dim | solution.py:151
  2.2 10.2 %all-to-all-start = ((bf16[32,8,1024]{2,1,0:T(8,128)(2,1)}), bf16[32,8,1024]{2,1,0:T(8,128)(2,1)S(1)}, u32[]{:S(2)}, u32[]{:S(2)}) async-start(bf16[32,8,1024]{2,1,0:T(8,128)(2,1)} %broadcast_in_dim.2), calls=%async_computation | async-start | bytes 1048576 | tf_op jit(solution)/shard_map/all_to_all | solution.py:153
  12.4 1.6 %stage.1 = (bf16[256,1024]{1,0:T(8,128)(2,1)S(1)}, bf16[256,1024]{1,0:T(8,128)(2,1)S(1)}, bf16[256,1024]{1,0:T(8,128)(2,1)S(1)}, bf16[256,1024]{1,0:T(8,128)(2,1)S(1)}) custom-call(bf16[1024,1024]{1,0:T(8,128)(2,1)} %points_ref), custom_call_target="tpu_custom_call" | custom-call | flops 10000000000 | bytes 4194304 | tf_op jit(solution)/shard_map/stage/pallas_call | solution.py:155
  14.0 1.9 %collective-permute-start.1 = (bf16[256,1024]{1,0:T(8,128)(2,1)S(1)}, bf16[256,1024]{1,0:T(8,128)(2,1)}, u32[]{:S(2)}, u32[]{:S(2)}) collective-permute-start(bf16[256,1024]{1,0:T(8,128)(2,1)S(1)} %get-tuple-element.15.refs_0_), channel_id=1, source_target_pairs={{0,1},{1,0},{2,3},{3,2},{4,5},{5,4},{6,7},{7,6},{8,9},{9,8},{10,11... | collective-permute-start | bytes 1572872 | tf_op jit(solution)/shard_map/ppermute | solution.py:166
  15.9 2.4 %collective-permute-start.2 = (bf16[256,1024]{1,0:T(8,128)(2,1)S(1)}, bf16[256,1024]{1,0:T(8,128)(2,1)}, u32[]{:S(2)}, u32[]{:S(2)}) collective-permute-start(bf16[256,1024]{1,0:T(8,128)(2,1)S(1)} %get-tuple-element.16.refs_1_), channel_id=1, source_target_pairs={{0,1},{1,0},{2,3},{3,2},{4,5},{5,4},{6,7},{7,6},{8,9},{9,8},{10,11... | collective-permute-start | bytes 1572872 | tf_op jit(solution)/shard_map/ppermute | solution.py:166
  18.3 1.9 %collective-permute-start.3 = (bf16[256,1024]{1,0:T(8,128)(2,1)S(1)}, bf16[256,1024]{1,0:T(8,128)(2,1)}, u32[]{:S(2)}, u32[]{:S(2)}) collective-permute-start(bf16[256,1024]{1,0:T(8,128)(2,1)S(1)} %get-tuple-element.17.refs_2_), channel_id=1, source_target_pairs={{0,1},{1,0},{2,3},{3,2},{4,5},{5,4},{6,7},{7,6},{8,9},{9,8},{10,11... | collective-permute-start | bytes 1572872 | tf_op jit(solution)/shard_map/ppermute | solution.py:166
  20.2 2.4 %collective-permute-start = (bf16[256,1024]{1,0:T(8,128)(2,1)S(1)}, bf16[256,1024]{1,0:T(8,128)(2,1)S(1)}, u32[]{:S(2)}, u32[]{:S(2)}) collective-permute-start(bf16[256,1024]{1,0:T(8,128)(2,1)S(1)} %get-tuple-element.18.refs_3_), channel_id=1, source_target_pairs={{0,1},{1,0},{2,3},{3,2},{4,5},{5,4},{6,7},{7,6},{8,9},{9,8},{10,11... | collective-permute-start | bytes 1572872 | tf_op jit(solution)/shard_map/ppermute | solution.py:166
  22.7 0.0 collective-permute-done.1.refs_5_
  22.7 0.0 collective-permute-done.2.refs_6_
  22.7 0.0 collective-permute-done.3.refs_7_
  22.7 1.5 %collective-permute-done.refs_4_ = bf16[256,1024]{1,0:T(8,128)(2,1)S(1)} collective-permute-done((bf16[256,1024]{1,0:T(8,128)(2,1)S(1)}, bf16[256,1024]{1,0:T(8,128)(2,1)S(1)}, u32[]{:S(2)}, u32[]{:S(2)}) %collective-permute-start) | collective-permute-done | bytes 524320 | tf_op jit(solution)/shard_map/ppermute | solution.py:166
  24.2 1.8 %all-to-all-done = bf16[32,8,1024]{2,1,0:T(8,128)(2,1)S(1)} async-done(((bf16[32,8,1024]{2,1,0:T(8,128)(2,1)}), bf16[32,8,1024]{2,1,0:T(8,128)(2,1)S(1)}, u32[]{:S(2)}, u32[]{:S(2)}) %all-to-all-start) | async-done | bytes 524320 | tf_op jit(solution)/shard_map/all_to_all | solution.py:153
  25.9 2.1 %local.1 = (f32[2,256,1024]{2,1,0:T(8,128)S(1)}, f32[16,16,128]{2,1,0:T(8,128)S(1)}, bf16[768,1024]{1,0:T(8,128)(2,1)S(1)}) custom-call(s32[1]{0:T(128)} %bitcast.core_ref, bf16[256,1024]{1,0:T(8,128)(2,1)S(1)} %bitcast.6, bf16[256,1024]{1,0:T(8,128)(2,1)S(1)} %get-tuple-element.15.refs_0_, bf16[256,1024]{1,0:T(8,128)(2,1)S(1)} %get-tuple-element.16.refs_1_, ...), custom_call_target="tpu_custom_call" | custom-call | tf_op jit(solution)/shard_map/local/pallas_call | solution.py:171
  28.1 18.7 %all_to_all.15.parts_ref = f32[16,16,128]{2,1,0:T(8,128)S(1)} all-to-all(f32[16,16,128]{2,1,0:T(8,128)S(1)} %get-tuple-element.20), channel_id=1, replica_groups=mesh['cent'=8,'chip'=32,'core'=2] {'core','cent'}, dimensions={0} | all-to-all | bytes 262144 | tf_op jit(solution)/shard_map/all_to_all | solution.py:185
  46.8 0.0 copy-start
  46.8 1.4 %sums.1 = (bf16[256,1152]{1,0:T(8,128)(2,1)S(1)}, f32[8,128]{1,0:T(8,128)}) custom-call(s32[1]{0:T(128)} %bitcast.core_ref, f32[2,256,1024]{2,1,0:T(8,128)S(1)} %get-tuple-element.19.logits_ref, f32[16,16,128]{2,1,0:T(8,128)S(1)} %all_to_all.15.parts_ref, bf16[256,1024]{1,0:T(8,128)(2,1)S(1)} %get-tuple-element.15.refs_0_, ...), custom_call_target="tpu_custom_call" | custom-call | tf_op jit(solution)/shard_map/sums/pallas_call | solution.py:187
  48.2 22.4 %all_to_all.16 = bf16[32,8,1152]{2,1,0:T(8,128)(2,1)S(1)} all-to-all(bf16[32,8,1152]{2,1,0:T(8,128)(2,1)S(1)} %bitcast.7), channel_id=1, replica_groups={{0,20,40,60,2,22,42,62,4,24,44,48,6,26,46,50,8,28,32,52,10,30,34,54,12,..., dimensions={0} | all-to-all | bytes 1179648 | tf_op jit(solution)/shard_map/all_to_all | solution.py:203
  70.5 0.0 copy-done
  70.5 0.8 %update.1 = bf16[8,1024]{1,0:T(8,128)(2,1)} custom-call(bf16[256,1152]{1,0:T(8,128)(2,1)S(1)} %bitcast.5, bf16[8,1024]{1,0:T(8,128)(2,1)S(1)} %copy-done), custom_call_target="tpu_custom_call" | custom-call | tf_op jit(solution)/shard_map/update/pallas_call | solution.py:205
Async XLA Ops:
  2.2 23.7 %all-to-all-start = ((bf16[32,8,1024]{2,1,0:T(8,128)(2,1)}), bf16[32,8,1024]{2,1,0:T(8,128)(2,1)S(1)}, u32[]{:S(2)}, u32[]{:S(2)}) async-start(bf16[32,8,1024]{2,1,0:T(8,128)(2,1)} %broadcast_in_dim.2), calls=%async_computation | async-start | bytes 1048576 | tf_op jit(solution)/shard_map/all_to_all | solution.py:153
  14.0 8.7 %collective-permute-start.1 = (bf16[256,1024]{1,0:T(8,128)(2,1)S(1)}, bf16[256,1024]{1,0:T(8,128)(2,1)}, u32[]{:S(2)}, u32[]{:S(2)}) collective-permute-start(bf16[256,1024]{1,0:T(8,128)(2,1)S(1)} %get-tuple-element.15.refs_0_), channel_id=1, source_target_pairs={{0,1},{1,0},{2,3},{3,2},{4,5},{5,4},{6,7},{7,6},{8,9},{9,8},{10,11... | collective-permute-start | bytes 1572872 | tf_op jit(solution)/shard_map/ppermute | solution.py:166
  15.9 6.8 %collective-permute-start.2 = (bf16[256,1024]{1,0:T(8,128)(2,1)S(1)}, bf16[256,1024]{1,0:T(8,128)(2,1)}, u32[]{:S(2)}, u32[]{:S(2)}) collective-permute-start(bf16[256,1024]{1,0:T(8,128)(2,1)S(1)} %get-tuple-element.16.refs_1_), channel_id=1, source_target_pairs={{0,1},{1,0},{2,3},{3,2},{4,5},{5,4},{6,7},{7,6},{8,9},{9,8},{10,11... | collective-permute-start | bytes 1572872 | tf_op jit(solution)/shard_map/ppermute | solution.py:166
  18.3 4.4 %collective-permute-start.3 = (bf16[256,1024]{1,0:T(8,128)(2,1)S(1)}, bf16[256,1024]{1,0:T(8,128)(2,1)}, u32[]{:S(2)}, u32[]{:S(2)}) collective-permute-start(bf16[256,1024]{1,0:T(8,128)(2,1)S(1)} %get-tuple-element.17.refs_2_), channel_id=1, source_target_pairs={{0,1},{1,0},{2,3},{3,2},{4,5},{5,4},{6,7},{7,6},{8,9},{9,8},{10,11... | collective-permute-start | bytes 1572872 | tf_op jit(solution)/shard_map/ppermute | solution.py:166
  20.2 3.9 %collective-permute-start = (bf16[256,1024]{1,0:T(8,128)(2,1)S(1)}, bf16[256,1024]{1,0:T(8,128)(2,1)S(1)}, u32[]{:S(2)}, u32[]{:S(2)}) collective-permute-start(bf16[256,1024]{1,0:T(8,128)(2,1)S(1)} %get-tuple-element.18.refs_3_), channel_id=1, source_target_pairs={{0,1},{1,0},{2,3},{3,2},{4,5},{5,4},{6,7},{7,6},{8,9},{9,8},{10,11... | collective-permute-start | bytes 1572872 | tf_op jit(solution)/shard_map/ppermute | solution.py:166
  46.8 23.7 %copy-start = (bf16[8,1024]{1,0:T(8,128)(2,1)S(1)}, bf16[8,1024]{1,0:T(8,128)(2,1)}, u32[]{:S(2)}) copy-start(bf16[8,1024]{1,0:T(8,128)(2,1)} %cent_ref.1) | copy-start | bytes 49156

commit v6 on v5

--- a/solution.py
+++ b/solution.py
@@ -114,13 +114,13 @@
     step = 2 * LANES
     for start in range(0, width, step):
         cols = pl.ds(start, step)
-        sums = jnp.dot(resp_ref[1, :, pl.ds(0, far)], other_ref[:, cols], preferred_element_type=F32)
-        sums += jnp.dot(resp_ref[1, :, pl.ds(far, points - far)], near_ref[:, cols], preferred_element_type=F32)
-        first = 0
+        sums, first = 0.0, 0
         for ref in own_refs:
             part = pl.ds(first, ref.shape[0])
             sums += jnp.dot(resp_ref[0, :, part], ref[:, cols], preferred_element_type=F32)
             first += ref.shape[0]
+        sums += jnp.dot(resp_ref[1, :, pl.ds(0, far)], other_ref[:, cols], preferred_element_type=F32)
+        sums += jnp.dot(resp_ref[1, :, pl.ds(far, points - far)], near_ref[:, cols], preferred_element_type=F32)
         send_ref[:, cols] = sums.astype(BF16)
 
 

time: 71.8 us -> 71.8 us (level)
  no operation moved by 1% of the time
where the time goes in v6:
time: 71.8 us; the launch traced here: 71.3 us
  blocking collectives  41.1 us (57%)
  starting transfers between devices  18.9 us (26%)
  Pallas kernels  5.83 us (8%)
  waiting for transfers between devices  3.26 us (5%)
  local copies, waits for them, and re-layouts  1.58 us (2%)
  between operations  0.72 us (1%)
    all_to_all x1, blocking collectives, body(): lax.all_to_all(send.reshape(chips, own, width + LANES), ('chip', 'core'),...  22.4 us
    all_to_all x1, blocking collectives, body(): parts = lax.all_to_all(part, ('core', 'cent'), 0, 0)  18.7 us
    all_to_all x1, starting transfers between devices, body(): lax.all_to_all(sent, ('chip', 'core'), 0, 0, axis_index_groups=order)  10.2 us
    ppermute x4, starting transfers between devices, body(): theirs = [lax.ppermute(x, 'core', [(0, 1), (1, 0)]) for x in mine]  8.66 us
    pallas_call x1, Pallas kernels, body(): pl.pallas_call(functools.partial(local_kernel, 2.0 / math.sqrt(width)), o...  2.14 us
    all_to_all x1, waiting for transfers between devices, body(): lax.all_to_all(sent, ('chip', 'core'), 0, 0, axis_index_groups=order)  1.77 us
    broadcast_in_dim x1, local copies, waits for them, and re-layouts, body(): sent = jnp.broadcast_to(centroids[None], (chips, own, width))  1.58 us
    pallas_call x1, Pallas kernels, body(): pl.pallas_call(stage_kernel, out_shape=[pltpu.VMEM((rows // PIECES, width...  1.55 us
  transfers between devices with their start and end apart: 5, of which 2 were waited for; matrix products, arithmetic and copies ran while one was open for 0% of the time, Pallas kernels for 2%

profile of v6, /device:TPU:6, one launch (start us, length us, event | category | flops | bytes accessed | tf_op | source)
XLA Modules:
  0.0 71.3 jit_solution(4417180289005536252)
XLA Ops:
  0.6 1.6 %broadcast_in_dim.2 = bf16[32,8,1024]{2,1,0:T(8,128)(2,1)} broadcast(bf16[8,1024]{1,0:T(8,128)(2,1)} %cent_ref.1), dimensions={1,2} | broadcast | bytes 540672 | tf_op jit(solution)/shard_map/broadcast_in_dim | solution.py:151
  2.2 10.2 %all-to-all-start = ((bf16[32,8,1024]{2,1,0:T(8,128)(2,1)}), bf16[32,8,1024]{2,1,0:T(8,128)(2,1)S(1)}, u32[]{:S(2)}, u32[]{:S(2)}) async-start(bf16[32,8,1024]{2,1,0:T(8,128)(2,1)} %broadcast_in_dim.2), calls=%async_computation | async-start | bytes 1048576 | tf_op jit(solution)/shard_map/all_to_all | solution.py:153
  12.4 1.6 %stage.1 = (bf16[256,1024]{1,0:T(8,128)(2,1)S(1)}, bf16[256,1024]{1,0:T(8,128)(2,1)S(1)}, bf16[256,1024]{1,0:T(8,128)(2,1)S(1)}, bf16[256,1024]{1,0:T(8,128)(2,1)S(1)}) custom-call(bf16[1024,1024]{1,0:T(8,128)(2,1)} %points_ref), custom_call_target="tpu_custom_call" | custom-call | flops 10000000000 | bytes 4194304 | tf_op jit(solution)/shard_map/stage/pallas_call | solution.py:155
  14.0 1.9 %collective-permute-start.1 = (bf16[256,1024]{1,0:T(8,128)(2,1)S(1)}, bf16[256,1024]{1,0:T(8,128)(2,1)}, u32[]{:S(2)}, u32[]{:S(2)}) collective-permute-start(bf16[256,1024]{1,0:T(8,128)(2,1)S(1)} %get-tuple-element.15.refs_0_), channel_id=1, source_target_pairs={{0,1},{1,0},{2,3},{3,2},{4,5},{5,4},{6,7},{7,6},{8,9},{9,8},{10,11... | collective-permute-start | bytes 1572872 | tf_op jit(solution)/shard_map/ppermute | solution.py:166
  15.9 2.4 %collective-permute-start.2 = (bf16[256,1024]{1,0:T(8,128)(2,1)S(1)}, bf16[256,1024]{1,0:T(8,128)(2,1)}, u32[]{:S(2)}, u32[]{:S(2)}) collective-permute-start(bf16[256,1024]{1,0:T(8,128)(2,1)S(1)} %get-tuple-element.16.refs_1_), channel_id=1, source_target_pairs={{0,1},{1,0},{2,3},{3,2},{4,5},{5,4},{6,7},{7,6},{8,9},{9,8},{10,11... | collective-permute-start | bytes 1572872 | tf_op jit(solution)/shard_map/ppermute | solution.py:166
  18.3 1.9 %collective-permute-start.3 = (bf16[256,1024]{1,0:T(8,128)(2,1)S(1)}, bf16[256,1024]{1,0:T(8,128)(2,1)}, u32[]{:S(2)}, u32[]{:S(2)}) collective-permute-start(bf16[256,1024]{1,0:T(8,128)(2,1)S(1)} %get-tuple-element.17.refs_2_), channel_id=1, source_target_pairs={{0,1},{1,0},{2,3},{3,2},{4,5},{5,4},{6,7},{7,6},{8,9},{9,8},{10,11... | collective-permute-start | bytes 1572872 | tf_op jit(solution)/shard_map/ppermute | solution.py:166
  20.2 2.4 %collective-permute-start = (bf16[256,1024]{1,0:T(8,128)(2,1)S(1)}, bf16[256,1024]{1,0:T(8,128)(2,1)S(1)}, u32[]{:S(2)}, u32[]{:S(2)}) collective-permute-start(bf16[256,1024]{1,0:T(8,128)(2,1)S(1)} %get-tuple-element.18.refs_3_), channel_id=1, source_target_pairs={{0,1},{1,0},{2,3},{3,2},{4,5},{5,4},{6,7},{7,6},{8,9},{9,8},{10,11... | collective-permute-start | bytes 1572872 | tf_op jit(solution)/shard_map/ppermute | solution.py:166
  22.7 0.0 collective-permute-done.1.refs_5_
  22.7 0.0 collective-permute-done.2.refs_6_
  22.7 0.0 collective-permute-done.3.refs_7_
  22.7 1.5 %collective-permute-done.refs_4_ = bf16[256,1024]{1,0:T(8,128)(2,1)S(1)} collective-permute-done((bf16[256,1024]{1,0:T(8,128)(2,1)S(1)}, bf16[256,1024]{1,0:T(8,128)(2,1)S(1)}, u32[]{:S(2)}, u32[]{:S(2)}) %collective-permute-start) | collective-permute-done | bytes 524320 | tf_op jit(solution)/shard_map/ppermute | solution.py:166
  24.2 1.8 %all-to-all-done = bf16[32,8,1024]{2,1,0:T(8,128)(2,1)S(1)} async-done(((bf16[32,8,1024]{2,1,0:T(8,128)(2,1)}), bf16[32,8,1024]{2,1,0:T(8,128)(2,1)S(1)}, u32[]{:S(2)}, u32[]{:S(2)}) %all-to-all-start) | async-done | bytes 524320 | tf_op jit(solution)/shard_map/all_to_all | solution.py:153
  25.9 2.1 %local.1 = (f32[2,256,1024]{2,1,0:T(8,128)S(1)}, f32[16,16,128]{2,1,0:T(8,128)S(1)}, bf16[768,1024]{1,0:T(8,128)(2,1)S(1)}) custom-call(s32[1]{0:T(128)} %bitcast.core_ref, bf16[256,1024]{1,0:T(8,128)(2,1)S(1)} %bitcast.6, bf16[256,1024]{1,0:T(8,128)(2,1)S(1)} %get-tuple-element.15.refs_0_, bf16[256,1024]{1,0:T(8,128)(2,1)S(1)} %get-tuple-element.16.refs_1_, ...), custom_call_target="tpu_custom_call" | custom-call | tf_op jit(solution)/shard_map/local/pallas_call | solution.py:171
  28.1 18.7 %all_to_all.15.parts_ref = f32[16,16,128]{2,1,0:T(8,128)S(1)} all-to-all(f32[16,16,128]{2,1,0:T(8,128)S(1)} %get-tuple-element.20), channel_id=1, replica_groups=mesh['cent'=8,'chip'=32,'core'=2] {'core','cent'}, dimensions={0} | all-to-all | bytes 262144 | tf_op jit(solution)/shard_map/all_to_all | solution.py:185
  46.8 0.0 copy-start
  46.8 1.4 %sums.1 = (bf16[256,1152]{1,0:T(8,128)(2,1)S(1)}, f32[8,128]{1,0:T(8,128)}) custom-call(s32[1]{0:T(128)} %bitcast.core_ref, f32[2,256,1024]{2,1,0:T(8,128)S(1)} %get-tuple-element.19.logits_ref, f32[16,16,128]{2,1,0:T(8,128)S(1)} %all_to_all.15.parts_ref, bf16[256,1024]{1,0:T(8,128)(2,1)S(1)} %get-tuple-element.15.refs_0_, ...), custom_call_target="tpu_custom_call" | custom-call | tf_op jit(solution)/shard_map/sums/pallas_call | solution.py:187
  48.2 22.4 %all_to_all.16 = bf16[32,8,1152]{2,1,0:T(8,128)(2,1)S(1)} all-to-all(bf16[32,8,1152]{2,1,0:T(8,128)(2,1)S(1)} %bitcast.7), channel_id=1, replica_groups={{0,20,40,60,2,22,42,62,4,24,44,48,6,26,46,50,8,28,32,52,10,30,34,54,12,..., dimensions={0} | all-to-all | bytes 1179648 | tf_op jit(solution)/shard_map/all_to_all | solution.py:203
  70.5 0.0 copy-done
  70.5 0.8 %update.1 = bf16[8,1024]{1,0:T(8,128)(2,1)} custom-call(bf16[256,1152]{1,0:T(8,128)(2,1)S(1)} %bitcast.5, bf16[8,1024]{1,0:T(8,128)(2,1)S(1)} %copy-done), custom_call_target="tpu_custom_call" | custom-call | tf_op jit(solution)/shard_map/update/pallas_call | solution.py:205
Async XLA Ops:
  2.2 23.7 %all-to-all-start = ((bf16[32,8,1024]{2,1,0:T(8,128)(2,1)}), bf16[32,8,1024]{2,1,0:T(8,128)(2,1)S(1)}, u32[]{:S(2)}, u32[]{:S(2)}) async-start(bf16[32,8,1024]{2,1,0:T(8,128)(2,1)} %broadcast_in_dim.2), calls=%async_computation | async-start | bytes 1048576 | tf_op jit(solution)/shard_map/all_to_all | solution.py:153
  14.0 8.7 %collective-permute-start.1 = (bf16[256,1024]{1,0:T(8,128)(2,1)S(1)}, bf16[256,1024]{1,0:T(8,128)(2,1)}, u32[]{:S(2)}, u32[]{:S(2)}) collective-permute-start(bf16[256,1024]{1,0:T(8,128)(2,1)S(1)} %get-tuple-element.15.refs_0_), channel_id=1, source_target_pairs={{0,1},{1,0},{2,3},{3,2},{4,5},{5,4},{6,7},{7,6},{8,9},{9,8},{10,11... | collective-permute-start | bytes 1572872 | tf_op jit(solution)/shard_map/ppermute | solution.py:166
  15.9 6.8 %collective-permute-start.2 = (bf16[256,1024]{1,0:T(8,128)(2,1)S(1)}, bf16[256,1024]{1,0:T(8,128)(2,1)}, u32[]{:S(2)}, u32[]{:S(2)}) collective-permute-start(bf16[256,1024]{1,0:T(8,128)(2,1)S(1)} %get-tuple-element.16.refs_1_), channel_id=1, source_target_pairs={{0,1},{1,0},{2,3},{3,2},{4,5},{5,4},{6,7},{7,6},{8,9},{9,8},{10,11... | collective-permute-start | bytes 1572872 | tf_op jit(solution)/shard_map/ppermute | solution.py:166
  18.3 4.4 %collective-permute-start.3 = (bf16[256,1024]{1,0:T(8,128)(2,1)S(1)}, bf16[256,1024]{1,0:T(8,128)(2,1)}, u32[]{:S(2)}, u32[]{:S(2)}) collective-permute-start(bf16[256,1024]{1,0:T(8,128)(2,1)S(1)} %get-tuple-element.17.refs_2_), channel_id=1, source_target_pairs={{0,1},{1,0},{2,3},{3,2},{4,5},{5,4},{6,7},{7,6},{8,9},{9,8},{10,11... | collective-permute-start | bytes 1572872 | tf_op jit(solution)/shard_map/ppermute | solution.py:166
  20.2 3.9 %collective-permute-start = (bf16[256,1024]{1,0:T(8,128)(2,1)S(1)}, bf16[256,1024]{1,0:T(8,128)(2,1)S(1)}, u32[]{:S(2)}, u32[]{:S(2)}) collective-permute-start(bf16[256,1024]{1,0:T(8,128)(2,1)S(1)} %get-tuple-element.18.refs_3_), channel_id=1, source_target_pairs={{0,1},{1,0},{2,3},{3,2},{4,5},{5,4},{6,7},{7,6},{8,9},{9,8},{10,11... | collective-permute-start | bytes 1572872 | tf_op jit(solution)/shard_map/ppermute | solution.py:166
  46.8 23.7 %copy-start = (bf16[8,1024]{1,0:T(8,128)(2,1)S(1)}, bf16[8,1024]{1,0:T(8,128)(2,1)}, u32[]{:S(2)}) copy-start(bf16[8,1024]{1,0:T(8,128)(2,1)} %cent_ref.1) | copy-start | bytes 49156
